TPU v7x, 32 devices: a whole 2x2x4 slice. The times are simulated.
32 devices in a mesh: groups: 1, expert: 8 (over z, y), tensor: 2 (over x), pair: 2 (over core).
Axes of the slice: x: 2, y: 2, z: 4, core: 2. Of those that a mesh axis runs over, the one named last changes fastest.
Arguments:
- tokens: bfloat16 [512, 3584], P(('groups', 'expert', 'tensor', 'pair')), may hold values from -6 to 6
- expert_ids: int32 [512, 8], P(('groups', 'expert', 'tensor', 'pair')), may hold values from 0 to 15, all different within a row; in each aligned block of 16 rows (0 to 15, 16 to 31, ...) at most 16 rows name the same one
- route_weight: float32 [512, 8], P(('groups', 'expert', 'tensor', 'pair')), may hold values from 0.05 to 0.5
- w_gate: bfloat16 [16, 3584, 1024], P(('expert', 'pair'), None, 'tensor'), may hold values from -0.09375 to 0.09375
- w_up: bfloat16 [16, 3584, 1024], P(('expert', 'pair'), None, 'tensor'), may hold values from -0.09375 to 0.09375
- w_down: bfloat16 [16, 1024, 3584], P(('expert', 'pair'), 'tensor'), may hold values from -0.1875 to 0.1875
- s_gate: bfloat16 [3584, 2048], P(None, ('tensor', 'pair')), may hold values from -0.09375 to 0.09375
- s_up: bfloat16 [3584, 2048], P(None, ('tensor', 'pair')), may hold values from -0.09375 to 0.09375
- s_down: bfloat16 [2048, 3584], P(('tensor', 'pair')), may hold values from -0.125 to 0.125
Outputs:
- moe_out: bfloat16 [512, 3584], P(('groups', 'expert', 'tensor', 'pair'))
Inputs may be any that keep to these rules, and one draw needn't show every extreme that they name: `expert_ids`: each row names 8 different experts. Among the 16 tokens of one device no expert is named by more than 16 tokens, and in every draw some expert is named by exactly 16 tokens of some device.
All inputs are finite; a program needn't handle non-finite values.
Results may differ from a plain program's by a relative error of at most 0.014.
Values may be sent and summed in bfloat16 or wider, within the bound.
No kernel may reach another device: no remote copies, remote signals or barrier semaphores. Data moves between devices by JAX's collectives and lax.ppermute only.
A program may use at most 64 MiB of HBM per device.

v0:
```python
import jax
import jax.numpy as jnp
from jax import lax
from jax.sharding import PartitionSpec as P


def per_device(tokens, expert_ids, route_weight, w_gate, w_up, w_down, s_gate, s_up, s_down):
    tok_rows, model_width = tokens.shape
    top_count = expert_ids.shape[1]
    owners = lax.axis_size(("expert", "pair"))
    row_piece = lax.all_gather(tokens, ("tensor", "pair"), axis=0, tiled=True)
    gate_part = jnp.dot(row_piece, s_gate, preferred_element_type=jnp.float32)
    upper_part = jnp.dot(row_piece, s_up, preferred_element_type=jnp.float32)
    shared_act = (jax.nn.silu(gate_part) * upper_part).astype(jnp.bfloat16)
    shared = lax.psum_scatter(
        jnp.dot(shared_act, s_down, preferred_element_type=jnp.float32).astype(jnp.bfloat16),
        ("tensor", "pair"),
        scatter_dimension=0,
        tiled=True,
    ).astype(jnp.float32)
    labels = jnp.arange(owners, dtype=jnp.int32)
    matches = expert_ids[:, :, None] == labels[None, None, :]
    chosen = jnp.any(matches, axis=1)
    weight = jnp.sum(jnp.where(matches, route_weight[:, :, None], 0.0), axis=1)
    slot_total = min(tok_rows, 2 * tok_rows * top_count // owners)
    position = jnp.cumsum(chosen.astype(jnp.int32), axis=0) - 1
    placement = chosen[:, :, None] & (
        position[:, :, None] == jnp.arange(slot_total, dtype=jnp.int32)[None, None, :]
    )
    outgoing = jnp.einsum(
        "tec,td->ecd", placement.astype(jnp.bfloat16), tokens, preferred_element_type=jnp.float32
    ).astype(jnp.bfloat16)
    n_expert = lax.axis_size("expert")
    n_tensor = lax.axis_size("tensor")
    n_pair = lax.axis_size("pair")
    copies = jnp.broadcast_to(
        outgoing.reshape(n_expert, 1, n_pair, slot_total, model_width),
        (n_expert, n_tensor, n_pair, slot_total, model_width),
    )
    copies = copies.reshape(n_expert * n_tensor * n_pair, slot_total, model_width)
    arrived = lax.all_to_all(
        copies, ("expert", "tensor", "pair"), split_axis=0, concat_axis=0, tiled=True
    )
    senders, slot_count, _ = arrived.shape
    flattened = arrived.reshape(senders * slot_count, model_width)
    gate_part = jnp.dot(flattened, w_gate[0], preferred_element_type=jnp.float32)
    upper_part = jnp.dot(flattened, w_up[0], preferred_element_type=jnp.float32)
    hidden = (jax.nn.silu(gate_part) * upper_part).astype(jnp.bfloat16)
    partial_value = jnp.dot(hidden, w_down[0], preferred_element_type=jnp.float32).astype(
        jnp.bfloat16
    )
    partial_value = partial_value.reshape(senders, slot_count, model_width)
    returning = lax.all_to_all(
        partial_value, ("expert", "tensor", "pair"), split_axis=0, concat_axis=0, tiled=True
    )
    grouped = returning.reshape(n_expert, n_tensor, n_pair, slot_count, model_width).astype(
        jnp.float32
    )
    summed = jnp.sum(grouped, axis=1).reshape(n_expert * n_pair, slot_count, model_width)
    returned = summed.astype(jnp.bfloat16)
    combine_scale = (placement.astype(jnp.float32) * weight[:, :, None]).reshape(
        tok_rows, owners * slot_total
    )
    routed = jnp.dot(
        combine_scale,
        returned.reshape(owners * slot_total, model_width).astype(jnp.float32),
        precision=lax.Precision.HIGHEST,
    )
    return (shared + routed).astype(jnp.bfloat16)


def solution(mesh):
    in_specs = (
        P(("groups", "expert", "tensor", "pair"), None),
        P(("groups", "expert", "tensor", "pair"), None),
        P(("groups", "expert", "tensor", "pair"), None),
        P(("expert", "pair"), None, "tensor"),
        P(("expert", "pair"), None, "tensor"),
        P(("expert", "pair"), "tensor", None),
        P(None, ("tensor", "pair")),
        P(None, ("tensor", "pair")),
        P(("tensor", "pair"), None),
    )
    out_specs = P(("groups", "expert", "tensor", "pair"), None)
    return jax.shard_map(
        per_device, mesh=mesh, in_specs=in_specs, out_specs=out_specs, check_vma=False
    )
```

profile of v0, /device:TPU:0, one launch (start us, length us, event | category | flops | bytes accessed | tf_op | source)
XLA Modules:
  0.0 213.8 jit_solution(6730240935387070470)
XLA Ops:
  6.5 0.8 copy.15
  7.3 0.1 fusion.31
  7.4 0.1 copy.16
  7.5 0.1 copy.17
  7.6 1.8 convolution_convert_fusion.1
  9.4 0.4 broadcast_in_dim.29
  9.9 0.0 copy-start.3
  9.9 90.1 %all_to_all.10 = bf16[32,16,3584]{2,1,0:T(8,128)(2,1)S(1)} all-to-all(bf16[32,16,3584]{2,1,0:T(8,128)(2,1)S(1)} %bitcast.38), channel_id=1, replica_groups=mesh['groups'=1,'expert'=8,'tensor'=2,'pair'=2] {'expert','tensor','pair'}, dimensions={0} | all-to-all | bytes 7340032 | tf_op jit(solution)/shard_map/all_to_all | solution.py:41
  99.9 1.8 copy-done
  101.8 2.0 fusion.5
  103.8 10.0 %convolution_convert_fusion = bf16[512,3584]{1,0:T(8,128)(2,1)} fusion(bf16[1,512,3584]{2,1,0:T(8,128)(2,1)} %param.14, bf16[512,3584]{1,0:T(8,128)(2,1)} %bitcast.43, bf16[1,3584,512]{2,1,0:T(8,128)(2,1)} %param.13, f32[512,512]{1,0:T(8,128)S(1)} %fusion.5), kind=kOutput, calls=%fused_computation | convolution fusion | flops 3761504256 | bytes 15728640 | tf_op jit(solution)/shard_map/dot_general | solution.py:49
  113.9 3.7 %all-to-all-start.1 = ((bf16[32,16,3584]{2,1,0:T(8,128)(2,1)}), bf16[32,16,3584]{2,1,0:T(8,128)(2,1)}, u32[]{:S(2)}, u32[]{:S(2)}) async-start(bf16[32,16,3584]{2,1,0:T(8,128)(2,1)} %bitcast.41), calls=%async_computation.2 | async-start | bytes 7340032 | tf_op jit(solution)/shard_map/all_to_all | solution.py:53
  117.5 0.0 reduce-scatter.2.cloned.1.call-start
  117.6 28.9 %all_gather.3 = bf16[64,3584]{1,0:T(8,128)(2,1)S(1)} all-gather(bf16[16,3584]{1,0:T(8,128)(2,1)S(1)} %copy-done.1), channel_id=1, replica_groups=mesh['groups'=1,'expert'=8,'tensor'=2,'pair'=2] {'tensor','pair'}, dimensions={0}, use_global_device_ids=true | all-gather | bytes 573440 | tf_op jit(solution)/shard_map/all_gather | solution.py:11
  146.5 2.8 %fusion.38 = f32[64,512]{1,0:T(8,128)S(1)} fusion(bf16[64,3584]{1,0:T(8,128)(2,1)S(1)} %all_gather.3, bf16[3584,512]{1,0:T(8,128)(2,1)} %param.15), kind=kOutput, calls=%fused_computation.39 | convolution fusion | flops 234881024 | bytes 4259840 | tf_op jit(solution)/shard_map/dot_general | solution.py:12
  149.3 5.4 %convolution_convert_fusion.2 = bf16[64,3584]{1,0:T(8,128)(2,1)} fusion(bf16[512,3584]{1,0:T(8,128)(2,1)} %param.17, bf16[64,3584]{1,0:T(8,128)(2,1)S(1)} %all_gather.3, bf16[3584,512]{1,0:T(8,128)(2,1)} %param.16, f32[64,512]{1,0:T(8,128)S(1)} %fusion.38), kind=kOutput, calls=%fused_computation.2 | convolution fusion | flops 470188032 | bytes 8388608 | tf_op jit(solution)/shard_map/dot_general | solution.py:16
  154.6 0.0 reduce-scatter.2.cloned.1.call-update
  154.7 0.1 copy.18
  154.7 0.1 select_reduce_fusion
  154.8 0.1 copy.19
  154.9 45.5 %all-to-all-done.1 = bf16[32,16,3584]{2,1,0:T(8,128)(2,1)} async-done(((bf16[32,16,3584]{2,1,0:T(8,128)(2,1)}), bf16[32,16,3584]{2,1,0:T(8,128)(2,1)}, u32[]{:S(2)}, u32[]{:S(2)}) %all-to-all-start.1) | async-done | bytes 3670048 | tf_op jit(solution)/shard_map/all_to_all | solution.py:53
  200.4 2.9 %reduce = bf16[8,2,16,3584]{3,2,1,0:T(8,128)(2,1)S(1)} reduce(bf16[8,2,2,16,3584]{4,3,2,1,0:T(8,128)(2,1)} %bitcast.8, bf16[]{:T(256)} %constant.23), dimensions={1}, to_apply=%region_4.5.clone | reduce | flops 917504 | bytes 5505026 | tf_op jit(solution)/shard_map/reduce_sum | solution.py:59
  203.3 0.0 reduce-scatter.2.cloned.1.call-done
  203.4 3.6 %fusion.1 = bf16[16,3584]{1,0:T(8,128)(2,1)} fusion(bf16[16,16,3584]{2,1,0:T(8,128)(2,1)S(1)} %bitcast.39, bf16[16,3584]{1,0:T(8,128)(2,1)} %reduce-scatter.2.cloned.1.call-done, f32[16,16]{0,1:T(8,128)S(1)} %copy.19, s32[16,16]{0,1:T(8,128)S(1)} %copy.17, pred[16,16]{0,1:T(8,128)(4,1)S(1)} %copy.16), kind=kOutput, calls=%fused_computation.5 | convolution fusion | flops 176345088 | bytes 2066688 | tf_op jit(solution)/shard_map/dot_general | solution.py:64
  (9 shorter events, 0.1 us)
Async XLA Ops:
  9.9 91.9 %copy-start.3 = (bf16[1,3584,512]{2,1,0:T(8,128)(2,1)S(1)}, bf16[1,3584,512]{2,1,0:T(8,128)(2,1)}, u32[]{:S(2)}) copy-start(bf16[1,3584,512]{2,1,0:T(8,128)(2,1)} %param.12) | copy-start | bytes 11010052
  99.9 1.8 copy-start
  113.9 3.7 %copy-start.1 = (bf16[16,3584]{1,0:T(8,128)(2,1)S(1)}, bf16[16,3584]{1,0:T(8,128)(2,1)}, u32[]{:S(2)}) copy-start(bf16[16,3584]{1,0:T(8,128)(2,1)} %param.9) | copy-start | bytes 344068
  113.9 86.5 %all-to-all-start.1 = ((bf16[32,16,3584]{2,1,0:T(8,128)(2,1)}), bf16[32,16,3584]{2,1,0:T(8,128)(2,1)}, u32[]{:S(2)}, u32[]{:S(2)}) async-start(bf16[32,16,3584]{2,1,0:T(8,128)(2,1)} %bitcast.41), calls=%async_computation.2 | async-start | bytes 7340032 | tf_op jit(solution)/shard_map/all_to_all | solution.py:53
  117.5 85.8 %reduce-scatter.2.cloned.1.call-start = ((), (), s32[]{:S(2)}) async-start(), calls=%async_computation.3 | async-start | bytes 573440 | tf_op jit(solution)/shard_map/reduce_scatter | solution.py:15
  149.2 5.4 %copy-start.2 = (f32[16,8]{0,1:T(8,128)S(1)}, f32[16,8]{0,1:T(8,128)}, u32[]{:S(2)}) copy-start(f32[16,8]{0,1:T(8,128)} %param.11) | copy-start | bytes 1540
Sparse Core Ops, SparseCore 0:
  154.8 26.5 reduce-scatter.1
where the time goes:
time: 214 us
  blocking collectives  119 us (56%)
  waiting for transfers between devices  45.5 us (21%)
  matrix products  25.7 us (12%)
  between operations  13.5 us (6%)
  starting transfers between devices  3.71 us (2%)
  local copies, waits for them, and re-layouts  3.32 us (2%)
  other arithmetic  3.18 us (1%)
    all_to_all x1, blocking collectives, per_device(): lax.all_to_all(copies, ('expert', 'tensor', 'pair'), split_axis=0, concat...  90.1 us
    all_to_all x1, waiting for transfers between devices, per_device(): lax.all_to_all(partial_value, ('expert', 'tensor', 'pair'), split_axis=0,...  45.5 us
    all_gather x1, blocking collectives, per_device(): row_piece = lax.all_gather(tokens, ('tensor', 'pair'), axis=0, tiled=True)  28.9 us
    dot_general x1, matrix products, per_device(): jnp.dot(hidden, w_down[0], preferred_element_type=jnp.float32)  10 us
    dot_general x1, matrix products, per_device(): jnp.dot(shared_act, s_down, preferred_element_type=jnp.float32)  5.38 us
  transfers between devices with their start and end apart: 2, of which 1 were waited for; matrix products, arithmetic and copies ran while one was open for 5% of the time, Pallas kernels for 0%

commit v1 on v0

v1 whole, which is shorter than its diff:
```python
import functools

import jax
import jax.numpy as jnp
from jax import lax
from jax.experimental import pallas as pl
from jax.experimental.pallas import tpu as pltpu
from jax.sharding import PartitionSpec as P

LANES = 128
VMEM_LIMIT = 48 * 1024 * 1024


def split_of(width):
    for parts in (4, 7, 2):
        if width % (parts * LANES) == 0:
            return parts
    return 1


def code_width(experts):
    return -(-2 * experts // LANES) * LANES


def pack_body(tokens_ref, ids_ref, weight_ref, out_ref):
    rows, model = tokens_ref.shape
    width = out_ref.shape[1] - model
    half = width // 2
    lane = lax.broadcasted_iota(jnp.int32, (rows, width), 1)
    place = jnp.where(lane < half, lane, lane - half)
    combine = jnp.zeros((rows, width), jnp.float32)
    for k in range(ids_ref.shape[1]):
        combine += jnp.where(place == ids_ref[:, k : k + 1], weight_ref[:, k : k + 1], 0.0)
    high = combine.astype(jnp.bfloat16).astype(jnp.float32)
    out_ref[:, :model] = tokens_ref[...]
    out_ref[:, model:] = jnp.where(lane < half, high, combine - high).astype(jnp.bfloat16)


def pack(tokens, expert_ids, route_weight, width):
    rows, model = tokens.shape
    return pl.pallas_call(
        pack_body,
        out_shape=jax.ShapeDtypeStruct((rows, model + width), jnp.bfloat16),
        name="pack",
    )(tokens, expert_ids, route_weight)


def ffn_body(steps, model, routed, adds, own_ref, *refs):
    refs = list(refs)
    xa_ref, xb_ref = refs.pop(0), refs.pop(0)
    if routed:
        ca_ref, cb_ref = refs.pop(0), refs.pop(0)
    wg_ref, wu_ref, wd_ref = refs.pop(0), refs.pop(0), refs.pop(0)
    if adds:
        sa_ref, sb_ref = refs.pop(0), refs.pop(0)
    oa_ref, ob_ref, gate, upper, hidden = refs
    rows = xa_ref.shape[0]
    step = pl.program_id(0)

    @pl.when(step < steps)
    def _():
        x = jnp.concatenate([xa_ref[...], xb_ref[...]], axis=0)
        g = jnp.dot(x, wg_ref[...], preferred_element_type=jnp.float32)
        u = jnp.dot(x, wu_ref[...], preferred_element_type=jnp.float32)

        @pl.when(step == 0)
        def _():
            gate[...] = g
            upper[...] = u

        @pl.when(step > 0)
        def _():
            gate[...] += g
            upper[...] += u

    @pl.when(step == steps - 1)
    def _():
        hidden[...] = (jax.nn.silu(gate[...]) * upper[...]).astype(jnp.bfloat16)

    @pl.when(step >= steps)
    def _():
        y = jnp.dot(hidden[...], wd_ref[...], preferred_element_type=jnp.float32)
        if routed:
            width = ca_ref.shape[1]
            lane = lax.broadcasted_iota(jnp.int32, (2 * rows, width), 1)
            mine = (lane == own_ref[0]) | (lane == own_ref[0] + width // 2)
            code = jnp.concatenate([ca_ref[...], cb_ref[...]], axis=0).astype(jnp.float32)
            y = y * jnp.sum(jnp.where(mine, code, 0.0), axis=1, keepdims=True)
        ya, yb = y[:rows], y[rows:]
        oa_ref[...] = ya.astype(oa_ref.dtype)
        ob_ref[...] = yb.astype(ob_ref.dtype)
        if adds:
            n = sa_ref.shape[0]
            oa_ref[:n, :] = (ya[:n] + sa_ref[...]).astype(oa_ref.dtype)
            ob_ref[:n, :] = (yb[:n] + sb_ref[...]).astype(ob_ref.dtype)


def ffn(xa, xb, own, w_gate, w_up, w_down, out_dtype, routed, extra=None, name="ffn"):
    rows = xa.shape[0]
    model, hid = w_gate.shape[-2:]
    steps = split_of(model)
    tile = model // steps
    lead = w_gate.ndim - 2
    first = lambda i, own: (0, jnp.minimum(i, steps - 1))
    second = lambda i, own: (0, jnp.maximum(i - steps, 0))
    w_first = lambda i, own: (0,) * lead + (jnp.minimum(i, steps - 1), 0)
    w_second = lambda i, own: (0,) * lead + (0, jnp.maximum(i - steps, 0))
    squeeze = (None,) * lead
    in_specs = [pl.BlockSpec((rows, tile), first)] * 2
    args = [xa, xb]
    if routed:
        width = xa.shape[1] - model
        in_specs += [pl.BlockSpec((rows, width), lambda i, own: (0, model // width))] * 2
        args += [xa, xb]
    in_specs += [pl.BlockSpec(squeeze + (tile, hid), w_first)] * 2
    in_specs += [pl.BlockSpec(squeeze + (hid, tile), w_second)]
    args += [w_gate, w_up, w_down]
    if extra is not None:
        in_specs += [pl.BlockSpec((extra[0].shape[0], tile), second)] * 2
        args += list(extra)
    out = jax.ShapeDtypeStruct((rows, model), out_dtype)
    return pl.pallas_call(
        functools.partial(ffn_body, steps, model, routed, extra is not None),
        out_shape=(out, out),
        grid_spec=pltpu.PrefetchScalarGridSpec(
            num_scalar_prefetch=1,
            grid=(2 * steps,),
            in_specs=in_specs,
            out_specs=[pl.BlockSpec((rows, tile), second)] * 2,
            scratch_shapes=[
                pltpu.VMEM((2 * rows, hid), jnp.float32),
                pltpu.VMEM((2 * rows, hid), jnp.float32),
                pltpu.VMEM((2 * rows, hid), jnp.bfloat16),
            ],
        ),
        compiler_params=pltpu.CompilerParams(vmem_limit_bytes=VMEM_LIMIT),
        cost_estimate=pl.CostEstimate(
            flops=12 * rows * model * hid,
            bytes_accessed=6 * model * hid + 8 * rows * model,
            transcendentals=2 * rows * hid,
        ),
        name=name,
    )(own, *args)


def sum_body(plan, n_in, *refs):
    ins, outs = refs[:n_in], refs[n_in:]
    for out_ref, terms in zip(outs, plan):
        total = None
        for index, start in terms:
            part = ins[index][start : start + out_ref.shape[0], :].astype(jnp.float32)
            total = part if total is None else total + part
        out_ref[...] = total.astype(out_ref.dtype)


def sums(arrays, plan, rows, dtypes, name):
    model = arrays[0].shape[1]
    parts = split_of(model)
    tile = model // parts
    return pl.pallas_call(
        functools.partial(sum_body, plan, len(arrays)),
        out_shape=tuple(jax.ShapeDtypeStruct((rows, model), d) for d in dtypes),
        grid=(parts,),
        in_specs=[pl.BlockSpec((a.shape[0], tile), lambda i: (0, i)) for a in arrays],
        out_specs=tuple(pl.BlockSpec((rows, tile), lambda i: (0, i)) for _ in dtypes),
        compiler_params=pltpu.CompilerParams(vmem_limit_bytes=VMEM_LIMIT),
        cost_estimate=pl.CostEstimate(
            flops=sum(a.size for a in arrays),
            bytes_accessed=4 * sum(a.size for a in arrays),
            transcendentals=0,
        ),
        name=name,
    )(*arrays)


def swap(size, by):
    if size & (size - 1) == 0:
        return [(i, i ^ by) for i in range(size)]
    return [(i, (i + by) % size) for i in range(size)]


def swap_back(size, by):
    return [(to, fro) for fro, to in swap(size, by)]


def per_device(tokens, expert_ids, route_weight, w_gate, w_up, w_down, s_gate, s_up, s_down):
    rows, model = tokens.shape
    n_expert = lax.axis_size("expert")
    n_tensor = lax.axis_size("tensor")
    n_pair = lax.axis_size("pair")
    assert n_pair == 2
    near = 2 if n_expert % 2 == 0 else 1
    far = n_expert // near

    def far_perm(by, back):
        table = swap_back(far, by) if back else swap(far, by)
        return [(a * near + c, b * near + c) for a, b in table for c in range(near)]

    def near_perm():
        return [(a * near + c, a * near + (c ^ 1)) for a in range(far) for c in range(near)]

    def go_far(t, by, back=False):
        return lax.ppermute(t, "expert", far_perm(by, back))

    def go_near(t):
        return lax.ppermute(t, "expert", near_perm())

    def go_tensor(t, by, back=False):
        return lax.ppermute(t, "tensor", (swap_back if back else swap)(n_tensor, by))

    def go_pair(t):
        return lax.ppermute(t, "pair", [(0, 1), (1, 0)])

    own = (lax.axis_index("expert") * n_pair + lax.axis_index("pair")).astype(jnp.int32)
    own = own.reshape(1)
    width = code_width(n_expert * n_pair)
    block = pack(tokens, expert_ids, route_weight, width)

    column = [block] + [go_far(block, k) for k in range(1, far)]
    blocks = {(0, 0): column}
    for j in range(1, n_tensor):
        blocks[j, 0] = [go_tensor(t, j) for t in column]
    if near == 2:
        blocks[0, 1] = [go_near(t) for t in column]
        for j in range(1, n_tensor):
            blocks[j, 1] = [
                go_near(blocks[j, 0][k]) if k % 2 == 0 else go_tensor(blocks[0, 1][k], j)
                for k in range(far)
            ]

    group = jnp.concatenate([blocks[j, 0][0] for j in range(n_tensor)], axis=0)
    shared = ffn(
        group, go_pair(group), own, s_gate, s_up, s_down, jnp.float32, False, name="shared"
    )

    mine, theirs = {}, {}
    for (j, i), group in blocks.items():
        group = jnp.concatenate(group, axis=0)
        extra = None
        if i == 0:
            extra = [s[j * rows : (j + 1) * rows] for s in shared]
        mine[j, i], other = ffn(
            group, go_pair(group), own, w_gate, w_up, w_down, jnp.bfloat16, True, extra,
            name="routed",
        )
        theirs[j, i] = go_pair(other)

    wide = [jnp.bfloat16] * far
    coming = {}
    if near == 2:
        for j in range(1, n_tensor):
            plan = [[(0, k * rows), (1, k * rows)] for k in range(far)]
            out = sums([mine[j, 1], theirs[j, 1]], plan, rows, wide, "sum_diagonal")
            coming[j] = [
                go_near(out[k]) if k % 2 == 0 else go_tensor(out[k], j, True) for k in range(far)
            ]
    returned = [[] for _ in range(far)]
    for j in range(1, n_tensor):
        arrays = [mine[j, 0], theirs[j, 0]]
        plan = [[(0, k * rows), (1, k * rows)] for k in range(far)]
        if near == 2:
            for k in range(0, far, 2):
                plan[k].append((len(arrays), 0))
                arrays.append(coming[j][k])
        out = sums(arrays, plan, rows, wide, "sum_tensor")
        for k in range(far):
            returned[k].append(go_tensor(out[k], j, True))
    if near == 2:
        arrays = [mine[0, 1], theirs[0, 1]]
        plan = [[(0, k * rows), (1, k * rows)] for k in range(far)]
        for j in range(1, n_tensor):
            for k in range(1, far, 2):
                plan[k].append((len(arrays), 0))
                arrays.append(coming[j][k])
        out = sums(arrays, plan, rows, wide, "sum_near")
        for k in range(far):
            returned[k].append(go_near(out[k]))
    arrays = [mine[0, 0], theirs[0, 0]]
    plan = [[(0, k * rows), (1, k * rows)] for k in range(far)]
    for k in range(far):
        for t in returned[k]:
            plan[k].append((len(arrays), 0))
            arrays.append(t)
    out = sums(arrays, plan, rows, [jnp.float32] + wide[1:], "sum_column")
    last = [out[0]] + [go_far(out[k], k, True) for k in range(1, far)]
    return sums(last, [[(n, 0) for n in range(far)]], rows, [jnp.bfloat16], "sum_far")[0]


def solution(mesh):
    in_specs = (
        P(("groups", "expert", "tensor", "pair"), None),
        P(("groups", "expert", "tensor", "pair"), None),
        P(("groups", "expert", "tensor", "pair"), None),
        P(("expert", "pair"), None, "tensor"),
        P(("expert", "pair"), None, "tensor"),
        P(("expert", "pair"), "tensor", None),
        P(None, ("tensor", "pair")),
        P(None, ("tensor", "pair")),
        P(("tensor", "pair"), None),
    )
    out_specs = P(("groups", "expert", "tensor", "pair"), None)
    return jax.shard_map(
        per_device, mesh=mesh, in_specs=in_specs, out_specs=out_specs, check_vma=False
    )
```

time: 214 us -> 144 us (0.67)
  blocking collectives: 119 us -> 0 us
  Pallas kernels: 0 us -> 43.9 us
  starting transfers between devices: 3.71 us -> 35.9 us
  matrix products: 25.7 us -> 0 us
  between operations: 13.5 us -> 0.26 us
  waiting for transfers between devices: 45.5 us -> 57.9 us
    all_to_all x1 -> x0, blocking collectives: 90.1 us -> none  [per_device(): lax.all_to_all(copies, ('expert', 'tensor', 'pair'), split_axis=0, concat...]
    ppermute x0 -> x39, waiting for transfers between devices: none -> 57.9 us  [the longest x12 25.4 us: go_tensor(): lax.ppermute(t, 'tensor', (swap_back if back else swap)(n_tensor, by))]
    all_to_all x1 -> x0, waiting for transfers between devices: 45.5 us -> none  [per_device(): lax.all_to_all(partial_value, ('expert', 'tensor', 'pair'), split_axis=0,...]
    pallas_call x0 -> x11, Pallas kernels: none -> 43.9 us  [the longest x5 39.1 us: ffn(): pl.pallas_call(functools.partial(ffn_body, steps, model, routed, extra is...]
    ppermute x0 -> x39, starting transfers between devices: none -> 35.9 us  [the longest x12 15.3 us: go_near(): return lax.ppermute(t, 'expert', near_perm())]
    all_gather x1 -> x0, blocking collectives: 28.9 us -> none  [per_device(): row_piece = lax.all_gather(tokens, ('tensor', 'pair'), axis=0, tiled=True)]
    dot_general x6 -> x0, matrix products: 25.7 us -> none  [the longest x1 10 us: per_device(): jnp.dot(hidden, w_down[0], preferred_element_type=jnp.float32)]
    all_to_all x1 -> x0, starting transfers between devices: 3.67 us -> none  [per_device(): lax.all_to_all(partial_value, ('expert', 'tensor', 'pair'), split_axis=0,...]
  transfers between devices with their start and end apart: 2 -> 39, of which waited for: 1 -> 20; matrix products, arithmetic and copies ran while one was open for 5% -> 2% of each run, Pallas kernels for 0% -> 28%
where the time goes in v1:
time: 144 us; the launch traced here: 143 us
  waiting for transfers between devices  57.9 us (40%)
  Pallas kernels  43.9 us (30%)
  starting transfers between devices  35.9 us (25%)
  local copies, waits for them, and re-layouts  2.94 us (2%)
  other arithmetic  2 us (1%)
    pallas_call x5, Pallas kernels, ffn(): pl.pallas_call(functools.partial(ffn_body, steps, model, routed, extra is...  39.1 us
    ppermute x12, waiting for transfers between devices, go_tensor(): lax.ppermute(t, 'tensor', (swap_back if back else swap)(n_tensor, by))  25.4 us
    ppermute x12, waiting for transfers between devices, go_near(): return lax.ppermute(t, 'expert', near_perm())  18.7 us
    ppermute x12, starting transfers between devices, go_near(): return lax.ppermute(t, 'expert', near_perm())  15.3 us
    ppermute x6, waiting for transfers between devices, go_far(): return lax.ppermute(t, 'expert', far_perm(by, back))  13.8 us
    ppermute x12, starting transfers between devices, go_tensor(): lax.ppermute(t, 'tensor', (swap_back if back else swap)(n_tensor, by))  10.1 us
    ppermute x6, starting transfers between devices, go_far(): return lax.ppermute(t, 'expert', far_perm(by, back))  8.84 us
    pallas_call x5, Pallas kernels, sums(): pl.pallas_call(functools.partial(sum_body, plan, len(arrays)), out_shape=...  3.15 us
  transfers between devices with their start and end apart: 39, of which 20 were waited for; matrix products, arithmetic and copies ran while one was open for 2% of the time, Pallas kernels for 28%

profile of v1, /device:TPU:0, one launch (start us, length us, event | category | flops | bytes accessed | tf_op | source)
XLA Modules:
  0.0 142.9 jit_solution(2653705102692179123)
XLA Ops:
  2.7 1.7 %pack.1 = bf16[16,3712]{1,0:T(8,128)(2,1)} custom-call(bf16[16,3584]{1,0:T(8,128)(2,1)} %tokens_ref.1, s32[16,8]{1,0:T(8,128)} %copy.10.ids_ref, f32[16,8]{1,0:T(8,128)} %copy.11.weight_ref), custom_call_target="tpu_custom_call" | custom-call | tf_op jit(solution)/shard_map/pack/pallas_call | solution.py:41
  4.4 2.9 %collective-permute-start.4 = (bf16[16,3712]{1,0:T(8,128)(2,1)}, bf16[16,3712]{1,0:T(8,128)(2,1)S(1)}, u32[]{:S(2)}, u32[]{:S(2)}) collective-permute-start(bf16[16,3712]{1,0:T(8,128)(2,1)} %pack.1), channel_id=1, source_target_pairs={{0,2},{2,0},{1,3},{3,1},{4,6},{6,4},{5,7},{7,5},{8,10},{10,8},{9,1... | collective-permute-start | bytes 356360 | tf_op jit(solution)/shard_map/ppermute | solution.py:209
  8.9 2.6 %collective-permute-start.1 = (bf16[16,3712]{1,0:T(8,128)(2,1)}, bf16[16,3712]{1,0:T(8,128)(2,1)S(1)}, u32[]{:S(2)}, u32[]{:S(2)}) collective-permute-start(bf16[16,3712]{1,0:T(8,128)(2,1)} %pack.1), channel_id=1, source_target_pairs={{0,16},{4,20},{8,24},{12,28},{16,0},{20,4},{24,8},{28,12},{1,17},{... | collective-permute-start | bytes 356360 | tf_op jit(solution)/shard_map/ppermute | solution.py:203
  14.4 6.5 %collective-permute-done.1 = bf16[16,3712]{1,0:T(8,128)(2,1)S(1)} collective-permute-done((bf16[16,3712]{1,0:T(8,128)(2,1)}, bf16[16,3712]{1,0:T(8,128)(2,1)S(1)}, u32[]{:S(2)}, u32[]{:S(2)}) %collective-permute-start.1) | collective-permute-done | bytes 118816 | tf_op jit(solution)/shard_map/ppermute | solution.py:203
  21.9 1.6 %collective-permute-start.13 = (bf16[16,3712]{1,0:T(8,128)(2,1)S(1)}, bf16[16,3712]{1,0:T(8,128)(2,1)S(1)}, u32[]{:S(2)}, u32[]{:S(2)}) collective-permute-start(bf16[16,3712]{1,0:T(8,128)(2,1)S(1)} %collective-permute-done), channel_id=1, source_target_pairs={{0,4},{4,0},{8,12},{12,8},{16,20},{20,16},{24,28},{28,24},{1,5},{5... | collective-permute-start | bytes 356360 | tf_op jit(solution)/shard_map/ppermute | solution.py:206
  24.6 3.4 %collective-permute-done.13 = bf16[16,3712]{1,0:T(8,128)(2,1)S(1)} collective-permute-done((bf16[16,3712]{1,0:T(8,128)(2,1)S(1)}, bf16[16,3712]{1,0:T(8,128)(2,1)S(1)}, u32[]{:S(2)}, u32[]{:S(2)}) %collective-permute-start.13) | collective-permute-done | bytes 118816 | tf_op jit(solution)/shard_map/ppermute | solution.py:206
  29.5 3.3 %collective-permute-done.24 = bf16[16,3712]{1,0:T(8,128)(2,1)S(1)} collective-permute-done((bf16[16,3712]{1,0:T(8,128)(2,1)S(1)}, bf16[16,3712]{1,0:T(8,128)(2,1)S(1)}, u32[]{:S(2)}, u32[]{:S(2)}) %collective-permute-start.24) | collective-permute-done | bytes 118816 | tf_op jit(solution)/shard_map/ppermute | solution.py:206
  34.3 3.3 %collective-permute-done.16 = bf16[16,3712]{1,0:T(8,128)(2,1)S(1)} collective-permute-done((bf16[16,3712]{1,0:T(8,128)(2,1)S(1)}, bf16[16,3712]{1,0:T(8,128)(2,1)S(1)}, u32[]{:S(2)}, u32[]{:S(2)}) %collective-permute-start.16) | collective-permute-done | bytes 118816 | tf_op jit(solution)/shard_map/ppermute | solution.py:206
  38.2 5.5 %collective-permute-done.7 = bf16[16,3712]{1,0:T(8,128)(2,1)S(1)} collective-permute-done((bf16[16,3712]{1,0:T(8,128)(2,1)S(1)}, bf16[16,3712]{1,0:T(8,128)(2,1)S(1)}, u32[]{:S(2)}, u32[]{:S(2)}) %collective-permute-start.7) | collective-permute-done | bytes 118816 | tf_op jit(solution)/shard_map/ppermute | solution.py:209
  44.3 4.2 %collective-permute-done.9 = bf16[16,3712]{1,0:T(8,128)(2,1)S(1)} collective-permute-done((bf16[16,3712]{1,0:T(8,128)(2,1)S(1)}, bf16[16,3712]{1,0:T(8,128)(2,1)S(1)}, u32[]{:S(2)}, u32[]{:S(2)}) %collective-permute-start.9) | collective-permute-done | bytes 118816 | tf_op jit(solution)/shard_map/ppermute | solution.py:209
  49.2 5.0 %collective-permute-done.14 = bf16[16,3712]{1,0:T(8,128)(2,1)S(1)} collective-permute-done((bf16[16,3712]{1,0:T(8,128)(2,1)S(1)}, bf16[16,3712]{1,0:T(8,128)(2,1)S(1)}, u32[]{:S(2)}, u32[]{:S(2)}) %collective-permute-start.14) | collective-permute-done | bytes 118816 | tf_op jit(solution)/shard_map/ppermute | solution.py:209
  55.8 3.3 %collective-permute-done.15 = bf16[16,3712]{1,0:T(8,128)(2,1)S(1)} collective-permute-done((bf16[16,3712]{1,0:T(8,128)(2,1)S(1)}, bf16[16,3712]{1,0:T(8,128)(2,1)S(1)}, u32[]{:S(2)}, u32[]{:S(2)}) %collective-permute-start.15) | collective-permute-done | bytes 118816 | tf_op jit(solution)/shard_map/ppermute | solution.py:206
  59.6 4.3 %collective-permute-done.17 = bf16[16,3712]{1,0:T(8,128)(2,1)S(1)} collective-permute-done((bf16[16,3712]{1,0:T(8,128)(2,1)S(1)}, bf16[16,3712]{1,0:T(8,128)(2,1)S(1)}, u32[]{:S(2)}, u32[]{:S(2)}) %collective-permute-start.17) | collective-permute-done | bytes 118816 | tf_op jit(solution)/shard_map/ppermute | solution.py:209
  64.1 7.8 %shared.1 = (f32[32,3584]{1,0:T(8,128)S(1)}, f32[32,3584]{1,0:T(8,128)S(1)}) custom-call(s32[1]{0:T(128)} %bitcast.own_ref, bf16[32,3712]{1,0:T(8,128)(2,1)S(1)} %pad_maximum_fusion.1.refs_0_, bf16[32,3712]{1,0:T(8,128)(2,1)S(1)} %collective-permute-done.5.refs_1_, bf16[3584,512]{1,0:T(8,128)(2,1)S(1)} %copy-done.1, bf16[3584,512]{1,0:T(8,128)(2,1)} %refs_3_.1, ...), custom_call_target="tpu_custom_call" | custom-call | flops 704643072 | bytes 11927552 | tf_op jit(solution)/shard_map/shared/pallas_call | solution.py:122
  71.9 7.9 %routed.7 = (bf16[64,3584]{1,0:T(8,128)(2,1)S(1)}, bf16[64,3584]{1,0:T(8,128)(2,1)S(1)}) custom-call(s32[1]{0:T(128)} %bitcast.own_ref, bf16[64,3712]{1,0:T(8,128)(2,1)S(1)} %constant_dynamic-update-slice_fusion.8.refs_0_.refs_2_, bf16[64,3712]{1,0:T(8,128)(2,1)S(1)} %collective-permute-done.25.refs_1_.refs_3_, ...), custom_call_target="tpu_custom_call" | custom-call | flops 1409286144 | bytes 12845056 | tf_op jit(solution)/shard_map/routed/pallas_call | solution.py:122
  80.3 7.8 %routed.6 = (bf16[64,3584]{1,0:T(8,128)(2,1)S(1)}, bf16[64,3584]{1,0:T(8,128)(2,1)S(1)}) custom-call(s32[1]{0:T(128)} %bitcast.own_ref, bf16[64,3712]{1,0:T(8,128)(2,1)S(1)} %constant_dynamic-update-slice_fusion.4.refs_0_.refs_2_, bf16[64,3712]{1,0:T(8,128)(2,1)S(1)} %collective-permute-done.18.refs_1_.refs_3_, ...), custom_call_target="tpu_custom_call" | custom-call | flops 1409286144 | bytes 12845056 | tf_op jit(solution)/shard_map/routed/pallas_call | solution.py:122
  88.3 7.8 %routed.5 = (bf16[64,3584]{1,0:T(8,128)(2,1)S(1)}, bf16[64,3584]{1,0:T(8,128)(2,1)S(1)}) custom-call(s32[1]{0:T(128)} %bitcast.own_ref, bf16[64,3712]{1,0:T(8,128)(2,1)S(1)} %constant_dynamic-update-slice_fusion.refs_0_.refs_2_, bf16[64,3712]{1,0:T(8,128)(2,1)S(1)} %collective-permute-done.10.refs_1_.refs_3_, ...), custom_call_target="tpu_custom_call" | custom-call | flops 1409286144 | bytes 12845056 | tf_op jit(solution)/shard_map/routed/pallas_call | solution.py:122
  96.6 7.8 %routed.4 = (bf16[64,3584]{1,0:T(8,128)(2,1)S(1)}, bf16[64,3584]{1,0:T(8,128)(2,1)S(1)}) custom-call(s32[1]{0:T(128)} %bitcast.own_ref, bf16[64,3712]{1,0:T(8,128)(2,1)S(1)} %pad_maximum_fusion.refs_0_.refs_2_, bf16[64,3712]{1,0:T(8,128)(2,1)S(1)} %collective-permute-done.3.refs_1_.refs_3_, bf16[64,3712]{1,0:T(8,128)(2,1)S(1)} %pad_maximum_fusion.refs_0_.refs_2_, ...), custom_call_target="tpu_custom_call" | custom-call | flops 1409286144 | bytes 12845056 | tf_op jit(solution)/shard_map/routed/pallas_call | solution.py:122
  108.6 2.4 %collective-permute-done.27.refs_2_ = bf16[16,3584]{1,0:T(8,128)(2,1)S(1)} collective-permute-done((bf16[16,3584]{1,0:T(8,128)(2,1)S(1)}, bf16[16,3584]{1,0:T(8,128)(2,1)S(1)}, u32[]{:S(2)}, u32[]{:S(2)}) %collective-permute-start.27) | collective-permute-done | bytes 114720 | tf_op jit(solution)/shard_map/ppermute | solution.py:209
  120.1 1.9 %collective-permute-done.31.refs_5_ = bf16[16,3584]{1,0:T(8,128)(2,1)S(1)} collective-permute-done((bf16[16,3584]{1,0:T(8,128)(2,1)S(1)}, bf16[16,3584]{1,0:T(8,128)(2,1)S(1)}, u32[]{:S(2)}, u32[]{:S(2)}) %collective-permute-start.31) | collective-permute-done | bytes 114720 | tf_op jit(solution)/shard_map/ppermute | solution.py:206
  122.5 1.8 %collective-permute-done.33.refs_7_ = bf16[16,3584]{1,0:T(8,128)(2,1)S(1)} collective-permute-done((bf16[16,3584]{1,0:T(8,128)(2,1)S(1)}, bf16[16,3584]{1,0:T(8,128)(2,1)S(1)}, u32[]{:S(2)}, u32[]{:S(2)}) %collective-permute-start.33) | collective-permute-done | bytes 114720 | tf_op jit(solution)/shard_map/ppermute | solution.py:206
  125.9 1.8 %collective-permute-done.32.refs_6_ = bf16[16,3584]{1,0:T(8,128)(2,1)S(1)} collective-permute-done((bf16[16,3584]{1,0:T(8,128)(2,1)S(1)}, bf16[16,3584]{1,0:T(8,128)(2,1)S(1)}, u32[]{:S(2)}, u32[]{:S(2)}) %collective-permute-start.32) | collective-permute-done | bytes 114720 | tf_op jit(solution)/shard_map/ppermute | solution.py:209
  129.8 1.9 %collective-permute-start.36 = (bf16[16,3584]{1,0:T(8,128)(2,1)S(1)}, bf16[16,3584]{1,0:T(8,128)(2,1)S(1)}, u32[]{:S(2)}, u32[]{:S(2)}) collective-permute-start(bf16[16,3584]{1,0:T(8,128)(2,1)S(1)} %get-tuple-element.54), channel_id=1, source_target_pairs={{8,0},{12,4},{0,8},{4,12},{24,16},{28,20},{16,24},{20,28},{9,1},{1... | collective-permute-start | bytes 344072 | tf_op jit(solution)/shard_map/ppermute | solution.py:203
  135.3 6.2 %collective-permute-done.37.refs_2_ = bf16[16,3584]{1,0:T(8,128)(2,1)S(1)} collective-permute-done((bf16[16,3584]{1,0:T(8,128)(2,1)S(1)}, bf16[16,3584]{1,0:T(8,128)(2,1)S(1)}, u32[]{:S(2)}, u32[]{:S(2)}) %collective-permute-start.37) | collective-permute-done | bytes 114720 | tf_op jit(solution)/shard_map/ppermute | solution.py:203
  (86 shorter events, 39.9 us)
Async XLA Ops:
  4.4 8.9 %collective-permute-start.4 = (bf16[16,3712]{1,0:T(8,128)(2,1)}, bf16[16,3712]{1,0:T(8,128)(2,1)S(1)}, u32[]{:S(2)}, u32[]{:S(2)}) collective-permute-start(bf16[16,3712]{1,0:T(8,128)(2,1)} %pack.1), channel_id=1, source_target_pairs={{0,2},{2,0},{1,3},{3,1},{4,6},{6,4},{5,7},{7,5},{8,10},{10,8},{9,1... | collective-permute-start | bytes 356360 | tf_op jit(solution)/shard_map/ppermute | solution.py:209
  7.3 7.1 %collective-permute-start = (bf16[16,3712]{1,0:T(8,128)(2,1)}, bf16[16,3712]{1,0:T(8,128)(2,1)S(1)}, u32[]{:S(2)}, u32[]{:S(2)}) collective-permute-start(bf16[16,3712]{1,0:T(8,128)(2,1)} %pack.1), channel_id=1, source_target_pairs={{0,8},{4,12},{8,0},{12,4},{16,24},{20,28},{24,16},{28,20},{1,9},{5... | collective-permute-start | bytes 356360 | tf_op jit(solution)/shard_map/ppermute | solution.py:203
  8.9 12.0 %collective-permute-start.1 = (bf16[16,3712]{1,0:T(8,128)(2,1)}, bf16[16,3712]{1,0:T(8,128)(2,1)S(1)}, u32[]{:S(2)}, u32[]{:S(2)}) collective-permute-start(bf16[16,3712]{1,0:T(8,128)(2,1)} %pack.1), channel_id=1, source_target_pairs={{0,16},{4,20},{8,24},{12,28},{16,0},{20,4},{24,8},{28,12},{1,17},{... | collective-permute-start | bytes 356360 | tf_op jit(solution)/shard_map/ppermute | solution.py:203
  11.5 9.4 %collective-permute-start.2 = (bf16[16,3712]{1,0:T(8,128)(2,1)}, bf16[16,3712]{1,0:T(8,128)(2,1)S(1)}, u32[]{:S(2)}, u32[]{:S(2)}) collective-permute-start(bf16[16,3712]{1,0:T(8,128)(2,1)} %pack.1), channel_id=1, source_target_pairs={{0,24},{4,28},{8,16},{12,20},{16,8},{20,12},{24,0},{28,4},{1,25},{... | collective-permute-start | bytes 356360 | tf_op jit(solution)/shard_map/ppermute | solution.py:203
  11.7 12.3 %collective-permute-start.23 = (bf16[16,3712]{1,0:T(8,128)(2,1)}, bf16[16,3712]{1,0:T(8,128)(2,1)S(1)}, u32[]{:S(2)}, u32[]{:S(2)}) collective-permute-start(bf16[16,3712]{1,0:T(8,128)(2,1)} %pack.1), channel_id=1, source_target_pairs={{0,4},{4,0},{8,12},{12,8},{16,20},{20,16},{24,28},{28,24},{1,5},{5... | collective-permute-start | bytes 356360 | tf_op jit(solution)/shard_map/ppermute | solution.py:206
  14.3 49.7 %collective-permute-start.5 = (bf16[32,3712]{1,0:T(8,128)(2,1)S(1)}, bf16[32,3712]{1,0:T(8,128)(2,1)S(1)}, u32[]{:S(2)}, u32[]{:S(2)}) collective-permute-start(bf16[32,3712]{1,0:T(8,128)(2,1)S(1)} %pad_maximum_fusion.1.refs_0_), channel_id=1, source_target_pairs={{0,1},{1,0},{2,3},{3,2},{4,5},{5,4},{6,7},{7,6},{8,9},{9,8},{10,11... | collective-permute-start | bytes 712712 | tf_op jit(solution)/shard_map/ppermute | solution.py:212
  21.8 74.8 %collective-permute-start.3 = (bf16[64,3712]{1,0:T(8,128)(2,1)S(1)}, bf16[64,3712]{1,0:T(8,128)(2,1)S(1)}, u32[]{:S(2)}, u32[]{:S(2)}) collective-permute-start(bf16[64,3712]{1,0:T(8,128)(2,1)S(1)} %pad_maximum_fusion.refs_0_.refs_2_), channel_id=1, source_target_pairs={{0,1},{1,0},{2,3},{3,2},{4,5},{5,4},{6,7},{7,6},{8,9},{9,8},{10,11... | collective-permute-start | bytes 1425416 | tf_op jit(solution)/shard_map/ppermute | solution.py:212
  23.5 25.2 %collective-permute-start.12 = (bf16[16,3712]{1,0:T(8,128)(2,1)S(1)}, bf16[16,3712]{1,0:T(8,128)(2,1)S(1)}, u32[]{:S(2)}, u32[]{:S(2)}) collective-permute-start(bf16[16,3712]{1,0:T(8,128)(2,1)S(1)} %collective-permute-done.4), channel_id=1, source_target_pairs={{0,4},{4,0},{8,12},{12,8},{16,20},{20,16},{24,28},{28,24},{1,5},{5... | collective-permute-start | bytes 356360 | tf_op jit(solution)/shard_map/ppermute | solution.py:206
  24.0 20.2 %collective-permute-start.8 = (bf16[16,3712]{1,0:T(8,128)(2,1)S(1)}, bf16[16,3712]{1,0:T(8,128)(2,1)S(1)}, u32[]{:S(2)}, u32[]{:S(2)}) collective-permute-start(bf16[16,3712]{1,0:T(8,128)(2,1)S(1)} %collective-permute-done.1), channel_id=1, source_target_pairs={{0,2},{2,0},{1,3},{3,1},{4,6},{6,4},{5,7},{7,5},{8,10},{10,8},{9,1... | collective-permute-start | bytes 356360 | tf_op jit(solution)/shard_map/ppermute | solution.py:209
  44.2 27.7 %collective-permute-start.25 = (bf16[64,3712]{1,0:T(8,128)(2,1)S(1)}, bf16[64,3712]{1,0:T(8,128)(2,1)S(1)}, u32[]{:S(2)}, u32[]{:S(2)}) collective-permute-start(bf16[64,3712]{1,0:T(8,128)(2,1)S(1)} %constant_dynamic-update-slice_fusion.8.refs_0_.refs_2_), channel_id=1, source_target_pairs={{0,1},{1,0},{2,3},{3,2},{4,5},{5,4},{6,7},{7,6},{8,9},{9,8},{10,11... | collective-permute-start | bytes 1425416 | tf_op jit(solution)/shard_map/ppermute | solution.py:212
  48.5 39.8 %collective-permute-start.10 = (bf16[64,3712]{1,0:T(8,128)(2,1)S(1)}, bf16[64,3712]{1,0:T(8,128)(2,1)S(1)}, u32[]{:S(2)}, u32[]{:S(2)}) collective-permute-start(bf16[64,3712]{1,0:T(8,128)(2,1)S(1)} %constant_dynamic-update-slice_fusion.refs_0_.refs_2_), channel_id=1, source_target_pairs={{0,1},{1,0},{2,3},{3,2},{4,5},{5,4},{6,7},{7,6},{8,9},{9,8},{10,11... | collective-permute-start | bytes 1425416 | tf_op jit(solution)/shard_map/ppermute | solution.py:212
  63.9 16.4 %collective-permute-start.18 = (bf16[64,3712]{1,0:T(8,128)(2,1)S(1)}, bf16[64,3712]{1,0:T(8,128)(2,1)S(1)}, u32[]{:S(2)}, u32[]{:S(2)}) collective-permute-start(bf16[64,3712]{1,0:T(8,128)(2,1)S(1)} %constant_dynamic-update-slice_fusion.4.refs_0_.refs_2_), channel_id=1, source_target_pairs={{0,1},{1,0},{2,3},{3,2},{4,5},{5,4},{6,7},{7,6},{8,9},{9,8},{10,11... | collective-permute-start | bytes 1425416 | tf_op jit(solution)/shard_map/ppermute | solution.py:212
  79.8 27.2 %collective-permute-start.26 = (bf16[64,3584]{1,0:T(8,128)(2,1)S(1)}, bf16[64,3584]{1,0:T(8,128)(2,1)S(1)}, u32[]{:S(2)}, u32[]{:S(2)}) collective-permute-start(bf16[64,3584]{1,0:T(8,128)(2,1)S(1)} %get-tuple-element.43), channel_id=1, source_target_pairs={{0,1},{1,0},{2,3},{3,2},{4,5},{5,4},{6,7},{7,6},{8,9},{9,8},{10,11... | collective-permute-start | bytes 1376264 | tf_op jit(solution)/shard_map/ppermute | solution.py:212
  88.2 16.4 %collective-permute-start.19 = (bf16[64,3584]{1,0:T(8,128)(2,1)S(1)}, bf16[64,3584]{1,0:T(8,128)(2,1)S(1)}, u32[]{:S(2)}, u32[]{:S(2)}) collective-permute-start(bf16[64,3584]{1,0:T(8,128)(2,1)S(1)} %get-tuple-element.38), channel_id=1, source_target_pairs={{0,1},{1,0},{2,3},{3,2},{4,5},{5,4},{6,7},{7,6},{8,9},{9,8},{10,11... | collective-permute-start | bytes 1376264 | tf_op jit(solution)/shard_map/ppermute | solution.py:212
  96.1 18.8 %collective-permute-start.11 = (bf16[64,3584]{1,0:T(8,128)(2,1)S(1)}, bf16[64,3584]{1,0:T(8,128)(2,1)S(1)}, u32[]{:S(2)}, u32[]{:S(2)}) collective-permute-start(bf16[64,3584]{1,0:T(8,128)(2,1)S(1)} %get-tuple-element.36), channel_id=1, source_target_pairs={{0,1},{1,0},{2,3},{3,2},{4,5},{5,4},{6,7},{7,6},{8,9},{9,8},{10,11... | collective-permute-start | bytes 1376264 | tf_op jit(solution)/shard_map/ppermute | solution.py:212
  104.5 13.5 %collective-permute-start.6 = (bf16[64,3584]{1,0:T(8,128)(2,1)S(1)}, bf16[64,3584]{1,0:T(8,128)(2,1)S(1)}, u32[]{:S(2)}, u32[]{:S(2)}) collective-permute-start(bf16[64,3584]{1,0:T(8,128)(2,1)S(1)} %get-tuple-element.34), channel_id=1, source_target_pairs={{0,1},{1,0},{2,3},{3,2},{4,5},{5,4},{6,7},{7,6},{8,9},{9,8},{10,11... | collective-permute-start | bytes 1376264 | tf_op jit(solution)/shard_map/ppermute | solution.py:212
  105.6 7.4 %collective-permute-start.28 = (bf16[16,3584]{1,0:T(8,128)(2,1)S(1)}, bf16[16,3584]{1,0:T(8,128)(2,1)S(1)}, u32[]{:S(2)}, u32[]{:S(2)}) collective-permute-start(bf16[16,3584]{1,0:T(8,128)(2,1)S(1)} %get-tuple-element.45), channel_id=1, source_target_pairs={{2,0},{0,2},{3,1},{1,3},{6,4},{4,6},{7,5},{5,7},{10,8},{8,10},{11,... | collective-permute-start | bytes 344072 | tf_op jit(solution)/shard_map/ppermute | solution.py:209
  107.0 8.4 %collective-permute-start.20 = (bf16[16,3584]{1,0:T(8,128)(2,1)S(1)}, bf16[16,3584]{1,0:T(8,128)(2,1)S(1)}, u32[]{:S(2)}, u32[]{:S(2)}) collective-permute-start(bf16[16,3584]{1,0:T(8,128)(2,1)S(1)} %get-tuple-element.39), channel_id=1, source_target_pairs={{0,4},{4,0},{8,12},{12,8},{16,20},{20,16},{24,28},{28,24},{1,5},{5... | collective-permute-start | bytes 344072 | tf_op jit(solution)/shard_map/ppermute | solution.py:206
  115.0 7.0 %collective-permute-start.31 = (bf16[16,3584]{1,0:T(8,128)(2,1)S(1)}, bf16[16,3584]{1,0:T(8,128)(2,1)S(1)}, u32[]{:S(2)}, u32[]{:S(2)}) collective-permute-start(bf16[16,3584]{1,0:T(8,128)(2,1)S(1)} %get-tuple-element.48), channel_id=1, source_target_pairs={{0,4},{4,0},{8,12},{12,8},{16,20},{20,16},{24,28},{28,24},{1,5},{5... | collective-permute-start | bytes 344072 | tf_op jit(solution)/shard_map/ppermute | solution.py:206
  115.5 8.9 %collective-permute-start.33 = (bf16[16,3584]{1,0:T(8,128)(2,1)S(1)}, bf16[16,3584]{1,0:T(8,128)(2,1)S(1)}, u32[]{:S(2)}, u32[]{:S(2)}) collective-permute-start(bf16[16,3584]{1,0:T(8,128)(2,1)S(1)} %get-tuple-element.50), channel_id=1, source_target_pairs={{0,4},{4,0},{8,12},{12,8},{16,20},{20,16},{24,28},{28,24},{1,5},{5... | collective-permute-start | bytes 344072 | tf_op jit(solution)/shard_map/ppermute | solution.py:206
  117.0 8.6 %collective-permute-start.35 = (bf16[16,3584]{1,0:T(8,128)(2,1)S(1)}, bf16[16,3584]{1,0:T(8,128)(2,1)S(1)}, u32[]{:S(2)}, u32[]{:S(2)}) collective-permute-start(bf16[16,3584]{1,0:T(8,128)(2,1)S(1)} %get-tuple-element.52), channel_id=1, source_target_pairs={{0,4},{4,0},{8,12},{12,8},{16,20},{20,16},{24,28},{28,24},{1,5},{5... | collective-permute-start | bytes 344072 | tf_op jit(solution)/shard_map/ppermute | solution.py:206
  117.9 7.6 %collective-permute-start.22 = (bf16[16,3584]{1,0:T(8,128)(2,1)S(1)}, bf16[16,3584]{1,0:T(8,128)(2,1)S(1)}, u32[]{:S(2)}, u32[]{:S(2)}) collective-permute-start(bf16[16,3584]{1,0:T(8,128)(2,1)S(1)} %get-tuple-element.41), channel_id=1, source_target_pairs={{2,0},{0,2},{3,1},{1,3},{6,4},{4,6},{7,5},{5,7},{10,8},{8,10},{11,... | collective-permute-start | bytes 344072 | tf_op jit(solution)/shard_map/ppermute | solution.py:209
  131.7 9.8 %collective-permute-start.37 = (bf16[16,3584]{1,0:T(8,128)(2,1)S(1)}, bf16[16,3584]{1,0:T(8,128)(2,1)S(1)}, u32[]{:S(2)}, u32[]{:S(2)}) collective-permute-start(bf16[16,3584]{1,0:T(8,128)(2,1)S(1)} %get-tuple-element.55), channel_id=1, source_target_pairs={{16,0},{20,4},{24,8},{28,12},{0,16},{4,20},{8,24},{12,28},{17,1},{... | collective-permute-start | bytes 344072 | tf_op jit(solution)/shard_map/ppermute | solution.py:203
  132.9 8.7 %collective-permute-start.38 = (bf16[16,3584]{1,0:T(8,128)(2,1)S(1)}, bf16[16,3584]{1,0:T(8,128)(2,1)S(1)}, u32[]{:S(2)}, u32[]{:S(2)}) collective-permute-start(bf16[16,3584]{1,0:T(8,128)(2,1)S(1)} %get-tuple-element.56), channel_id=1, source_target_pairs={{24,0},{28,4},{16,8},{20,12},{8,16},{12,20},{0,24},{4,28},{25,1},{... | collective-permute-start | bytes 344072 | tf_op jit(solution)/shard_map/ppermute | solution.py:203
  (17 other events, 141.3 us)

commit v2 on v0

v2 whole, which is shorter than its diff:
```python
import functools

import jax
import jax.numpy as jnp
from jax import lax
from jax.experimental import pallas as pl
from jax.experimental.pallas import tpu as pltpu
from jax.sharding import PartitionSpec as P

LANES = 128
VMEM_LIMIT = 20 * 1024 * 1024
IN_VMEM = pl.BlockSpec(memory_space=pltpu.VMEM)


def split_of(width):
    for parts in (4, 7, 2):
        if width % (parts * LANES) == 0:
            return parts
    return 1


def params():
    return pltpu.CompilerParams(vmem_limit_bytes=VMEM_LIMIT)


def pack_body(tokens_ref, ids_ref, weight_ref, out_ref):
    rows, model = tokens_ref.shape
    width = out_ref.shape[1] - model
    half = width // 2
    line = lax.broadcasted_iota(jnp.int32, (width, rows), 0)
    place = jnp.where(line < half, line, line - half)
    combine = jnp.zeros((width, rows), jnp.float32)
    for k in range(ids_ref.shape[0]):
        combine += jnp.where(place == ids_ref[k : k + 1, :], weight_ref[k : k + 1, :], 0.0)
    high = combine.astype(jnp.bfloat16).astype(jnp.float32)
    code = jnp.where(line < half, high, combine - high)
    out_ref[:, :model] = tokens_ref[...]
    out_ref[:, model:] = code.T.astype(jnp.bfloat16)


def pack(tokens, expert_ids, route_weight, width):
    rows, model = tokens.shape
    return pl.pallas_call(
        pack_body,
        out_shape=jax.ShapeDtypeStruct((rows, model + width), jnp.bfloat16),
        in_specs=[IN_VMEM] * 3,
        out_specs=IN_VMEM,
        name="pack",
    )(tokens, expert_ids.T, route_weight.T)


def ffn_body(n_parts, with_shared, share_of, index_ref, *refs):
    parts, refs = refs[: 2 * n_parts], refs[2 * n_parts :]
    wg_ref, wu_ref, wd_ref = refs[:3]
    if with_shared:
        sg_ref, su_ref, sd_ref = refs[3:6]
    oa_ref, ob_ref, x_ref = refs[-3:]
    rows, model = oa_ref.shape
    start = 0
    for part in parts:
        x_ref[start : start + part.shape[0], :] = part[...]
        start += part.shape[0]
    x = x_ref[:, :model]

    def hidden(g_ref, u_ref):
        g = jnp.dot(x, g_ref[...], preferred_element_type=jnp.float32)
        u = jnp.dot(x, u_ref[...], preferred_element_type=jnp.float32)
        return (jax.nn.silu(g) * u).astype(jnp.bfloat16)

    h = hidden(wg_ref, wu_ref)
    width = x_ref.shape[1] - model
    lane = lax.broadcasted_iota(jnp.int32, (2 * rows, width), 1)
    mine = (lane == index_ref[0]) | (lane == index_ref[0] + width // 2)
    code = x_ref[:, model:].astype(jnp.float32)
    scale = jnp.sum(jnp.where(mine, code, 0.0), axis=1, keepdims=True)
    if with_shared:
        s = hidden(sg_ref, su_ref)
        row = lax.broadcasted_iota(jnp.int32, (2 * rows, 1), 0)
        share = share_of(row, rows, index_ref[1])
    steps = split_of(model)
    tile = model // steps
    for i in range(steps):
        at = slice(i * tile, (i + 1) * tile)
        y = jnp.dot(h, wd_ref[:, at], preferred_element_type=jnp.float32) * scale
        if with_shared:
            more = jnp.dot(s, sd_ref[:, at], preferred_element_type=jnp.float32)
            y = y + jnp.where(share, more, 0.0)
        oa_ref[:, at] = y[:rows].astype(oa_ref.dtype)
        ob_ref[:, at] = y[rows:].astype(ob_ref.dtype)


def ffn(own_parts, other_parts, index, weights, share_of, name):
    rows = sum(p.shape[0] for p in own_parts)
    wide = own_parts[0].shape[1]
    hid, model = weights[2].shape
    out = jax.ShapeDtypeStruct((rows, model), jnp.bfloat16)
    parts = [*own_parts, *other_parts]
    return pl.pallas_call(
        functools.partial(ffn_body, len(own_parts), len(weights) > 3, share_of),
        out_shape=(out, out),
        in_specs=[pl.BlockSpec(memory_space=pltpu.SMEM)] + [IN_VMEM] * (len(parts) + len(weights)),
        out_specs=(IN_VMEM, IN_VMEM),
        scratch_shapes=[pltpu.VMEM((2 * rows, wide), jnp.bfloat16)],
        compiler_params=params(),
        cost_estimate=pl.CostEstimate(
            flops=4 * rows * model * hid * len(weights),
            bytes_accessed=8 * rows * model,
            transcendentals=2 * rows * hid,
        ),
        name=name,
    )(index, *parts, *weights)


def sum_body(starts, *refs):
    out_ref = refs[-1]
    total = None
    for ref, start in zip(refs, starts):
        part = ref[start : start + out_ref.shape[0], :].astype(jnp.float32)
        total = part if total is None else total + part
    out_ref[...] = total.astype(out_ref.dtype)


def sums(terms, rows, dtype, name):
    arrays = [a for a, _ in terms]
    model = arrays[0].shape[1]
    return pl.pallas_call(
        functools.partial(sum_body, [s for _, s in terms]),
        out_shape=jax.ShapeDtypeStruct((rows, model), dtype),
        in_specs=[IN_VMEM] * len(arrays),
        out_specs=IN_VMEM,
        compiler_params=params(),
        cost_estimate=pl.CostEstimate(
            flops=rows * model * len(arrays),
            bytes_accessed=2 * rows * model * len(arrays),
            transcendentals=0,
        ),
        name=name,
    )(*arrays)


def table(size, by):
    if size & (size - 1) == 0:
        return [i ^ by for i in range(size)]
    return [(i + by) % size for i in range(size)]


class Routes:
    axes = ("expert", "tensor", "pair")

    def __init__(self, n_expert, n_tensor, n_pair):
        self.sizes = (n_expert, n_tensor, n_pair)
        self.near = 2 if n_expert % 2 == 0 else 1
        self.far = n_expert // self.near
        self.colored = n_tensor == 2 and self.near == 2 and n_pair == 2

    def build(self, move):
        n_expert, n_tensor, n_pair = self.sizes
        out = []
        for e in range(n_expert):
            for t in range(n_tensor):
                for c in range(n_pair):
                    f, n = divmod(e, self.near)
                    f, n, t2, c2 = move(f, n, t, c)
                    out.append(((f * self.near + n) * n_tensor + t2) * n_pair + c2)
        return out

    def along_far(self, by):
        go = table(self.far, by)
        return self.build(lambda f, n, t, c: (go[f], n, t, c))

    def along_tensor(self, by):
        go = table(self.sizes[1], by)
        return self.build(lambda f, n, t, c: (f, n, go[t], c))

    def along_near(self):
        return self.build(lambda f, n, t, c: (f, n ^ 1, t, c))

    def other_core(self):
        return self.build(lambda f, n, t, c: (f, n, t, c ^ 1))

    def first(self):
        if self.colored:
            return [
                self.build(lambda f, n, t, c: (f, n, t ^ 1, c) if c == 0 else (f, n ^ 1, t, c))
            ]
        return [self.along_tensor(j) for j in range(1, self.sizes[1])]

    def second(self):
        if self.colored:
            return self.build(lambda f, n, t, c: (f, n ^ 1, t, c) if c == 0 else (f, n, t ^ 1, c))
        return self.along_near() if self.near == 2 else None

    def send(self, x, route):
        return lax.ppermute(x, self.axes, list(enumerate(route)))

    def send_back(self, x, route):
        return lax.ppermute(x, self.axes, [(to, fro) for fro, to in enumerate(route)])


def per_device(tokens, expert_ids, route_weight, w_gate, w_up, w_down, s_gate, s_up, s_down):
    rows, model = tokens.shape
    n_expert = lax.axis_size("expert")
    n_tensor = lax.axis_size("tensor")
    n_pair = lax.axis_size("pair")
    assert n_pair == 2
    routes = Routes(n_expert, n_tensor, n_pair)
    far = routes.far
    cross = routes.other_core()
    first, second = routes.first(), routes.second()

    core = lax.axis_index("pair")
    index = jnp.stack([lax.axis_index("expert") * n_pair + core, core]).astype(jnp.int32)
    pin = lambda w: pltpu.with_memory_space_constraint(w, pltpu.VMEM)
    routed_weights = [pin(w.reshape(w.shape[-2:])) for w in (w_gate, w_up, w_down)]
    shared_weights = [pin(w) for w in (s_gate, s_up, s_down)]
    width = -(-2 * n_expert * n_pair // LANES) * LANES
    block = pack(tokens, expert_ids, route_weight, width)

    def share_of(row, half, core):
        other = row >= half
        row = jnp.where(other, row - half, row)
        place = row // rows
        if not routes.colored:
            return place < n_tensor
        turn = jnp.where(other, 1 - core, core)
        return (place == 0) | (place == 1 + turn)

    order = list(range(far - 1, -1, -1))
    far_route = {k: routes.along_far(k) for k in range(1, far)}
    mine, theirs, head = {}, {}, {}
    for k in order:
        head[k] = routes.send(block, far_route[k]) if k else block
    for k in order:
        parts = [head[k]] + [routes.send(head[k], r) for r in first]
        if second is not None:
            parts.append(routes.send(jnp.concatenate(parts, axis=0), second))
        others = [routes.send(p, cross) for p in parts]
        weights = routed_weights + (shared_weights if k == 0 else [])
        mine[k], other = ffn(parts, others, index, weights, share_of, "ffn_%d" % k)
        theirs[k] = routes.send(other, cross)

    last = []
    for k in order:
        pair = [mine[k], theirs[k]]
        many = len(first) + 1
        terms = lambda start, more: [(a, start) for a in pair] + more
        came = []
        if second is not None:
            out = sums(terms(many * rows, []), many * rows, jnp.bfloat16, "sum_second")
            came = [routes.send_back(out, second)]
        home = []
        for j, r in enumerate(first):
            at = (j + 1) * rows
            out = sums(terms(at, [(a, at) for a in came]), rows, jnp.bfloat16, "sum_first")
            home.append(routes.send_back(out, r))
        dtype = jnp.bfloat16 if k else jnp.float32
        out = sums(terms(0, [(a, 0) for a in came + home]), rows, dtype, "sum_far")
        last.append(routes.send_back(out, far_route[k]) if k else out)
    return sums([(a, 0) for a in last], rows, jnp.bfloat16, "sum_last")


def solution(mesh):
    in_specs = (
        P(("groups", "expert", "tensor", "pair"), None),
        P(("groups", "expert", "tensor", "pair"), None),
        P(("groups", "expert", "tensor", "pair"), None),
        P(("expert", "pair"), None, "tensor"),
        P(("expert", "pair"), None, "tensor"),
        P(("expert", "pair"), "tensor", None),
        P(None, ("tensor", "pair")),
        P(None, ("tensor", "pair")),
        P(("tensor", "pair"), None),
    )
    out_specs = P(("groups", "expert", "tensor", "pair"), None)
    return jax.shard_map(
        per_device, mesh=mesh, in_specs=in_specs, out_specs=out_specs, check_vma=False
    )
```

time: 214 us -> 85.4 us (0.40)
  blocking collectives: 119 us -> 0 us
  starting transfers between devices: 3.71 us -> 34.3 us
  matrix products: 25.7 us -> 0 us
  waiting for transfers between devices: 45.5 us -> 27.7 us
  Pallas kernels: 0 us -> 13.8 us
  between operations: 13.5 us -> 0.23 us
  local copies, waits for them, and re-layouts: 3.32 us -> 8.05 us
    all_to_all x1 -> x0, blocking collectives: 90.1 us -> none  [per_device(): lax.all_to_all(copies, ('expert', 'tensor', 'pair'), split_axis=0, concat...]
    all_to_all x1 -> x0, waiting for transfers between devices: 45.5 us -> none  [per_device(): lax.all_to_all(partial_value, ('expert', 'tensor', 'pair'), split_axis=0,...]
    ppermute x0 -> x38, starting transfers between devices: none -> 34.3 us  [the longest x27 19.2 us: send(): return lax.ppermute(x, self.axes, list(enumerate(route)))]
    all_gather x1 -> x0, blocking collectives: 28.9 us -> none  [per_device(): row_piece = lax.all_gather(tokens, ('tensor', 'pair'), axis=0, tiled=True)]
    ppermute x0 -> x38, waiting for transfers between devices: none -> 27.7 us  [the longest x11 14.9 us: send_back(): lax.ppermute(x, self.axes, [(to, fro) for fro, to in enumerate(route)])]
    dot_general x6 -> x0, matrix products: 25.7 us -> none  [the longest x1 10 us: per_device(): jnp.dot(hidden, w_down[0], preferred_element_type=jnp.float32)]
    pallas_call x0 -> x18, Pallas kernels: none -> 13.8 us  [the longest x4 10.8 us: ffn(): pl.pallas_call(functools.partial(ffn_body, len(own_parts), len(weights) >...]
    unnamed x10 -> x20, local copies, waits for them, and re-layouts: 2.68 us -> 8.05 us
  transfers between devices with their start and end apart: 2 -> 38, of which waited for: 1 -> 11; matrix products, arithmetic and copies ran while one was open for 5% -> 1% of each run, Pallas kernels for 0% -> 13%
where the time goes in v2:
time: 85.4 us; the launch traced here: 85.1 us
  starting transfers between devices  34.3 us (40%)
  waiting for transfers between devices  27.7 us (32%)
  Pallas kernels  13.8 us (16%)
  local copies, waits for them, and re-layouts  8.05 us (9%)
  other arithmetic  1.05 us (1%)
    ppermute x27, starting transfers between devices, send(): return lax.ppermute(x, self.axes, list(enumerate(route)))  19.2 us
    ppermute x11, starting transfers between devices, send_back(): lax.ppermute(x, self.axes, [(to, fro) for fro, to in enumerate(route)])  15.1 us
    ppermute x11, waiting for transfers between devices, send_back(): lax.ppermute(x, self.axes, [(to, fro) for fro, to in enumerate(route)])  14.9 us
    ppermute x27, waiting for transfers between devices, send(): return lax.ppermute(x, self.axes, list(enumerate(route)))  12.8 us
    pallas_call x4, Pallas kernels, ffn(): pl.pallas_call(functools.partial(ffn_body, len(own_parts), len(weights) >...  10.8 us
    unnamed x20, local copies, waits for them, and re-layouts  8.05 us
  transfers between devices with their start and end apart: 38, of which 11 were waited for; matrix products, arithmetic and copies ran while one was open for 1% of the time, Pallas kernels for 13%

profile of v2, /device:TPU:0, one launch (start us, length us, event | category | flops | bytes accessed | tf_op | source)
XLA Modules:
  0.0 85.1 jit_solution(14737289939403581528)
XLA Ops:
  0.0 1.7 %pack.1.refs_0_ = bf16[16,3712]{1,0:T(8,128)(2,1)} custom-call(bf16[16,3584]{1,0:T(8,128)(2,1)} %tokens_ref.1, s32[8,16]{1,0:T(8,128)} %bitcast.19, f32[8,16]{1,0:T(8,128)} %bitcast.20), custom_call_target="tpu_custom_call" | custom-call | tf_op jit(solution)/shard_map/pack/pallas_call | solution.py:43
  1.7 5.0 %collective-permute-start = (bf16[16,3712]{1,0:T(8,128)(2,1)}, bf16[16,3712]{1,0:T(8,128)(2,1)S(1)}, u32[]{:S(2)}, u32[]{:S(2)}) collective-permute-start(bf16[16,3712]{1,0:T(8,128)(2,1)} %pack.1.refs_0_), channel_id=1, source_target_pairs={{0,24},{1,25},{2,26},{3,27},{4,28},{5,29},{6,30},{7,31},{8,16},{9,... | collective-permute-start | bytes 356360 | tf_op jit(solution)/shard_map/ppermute | solution.py:194
  7.3 3.8 %collective-permute-done.refs_0_ = bf16[16,3712]{1,0:T(8,128)(2,1)S(1)} collective-permute-done((bf16[16,3712]{1,0:T(8,128)(2,1)}, bf16[16,3712]{1,0:T(8,128)(2,1)S(1)}, u32[]{:S(2)}, u32[]{:S(2)}) %collective-permute-start) | collective-permute-done | bytes 118816 | tf_op jit(solution)/shard_map/ppermute | solution.py:194
  11.1 1.7 %collective-permute-start.1 = (bf16[16,3712]{1,0:T(8,128)(2,1)S(1)}, bf16[16,3712]{1,0:T(8,128)(2,1)S(1)}, u32[]{:S(2)}, u32[]{:S(2)}) collective-permute-start(bf16[16,3712]{1,0:T(8,128)(2,1)S(1)} %collective-permute-done.refs_0_), channel_id=1, source_target_pairs={{0,2},{1,5},{2,0},{3,7},{4,6},{5,1},{6,4},{7,3},{8,10},{9,13},{10,... | collective-permute-start | bytes 356360 | tf_op jit(solution)/shard_map/ppermute | solution.py:194
  13.1 3.8 %collective-permute-done.10.refs_0_ = bf16[16,3712]{1,0:T(8,128)(2,1)S(1)} collective-permute-done((bf16[16,3712]{1,0:T(8,128)(2,1)}, bf16[16,3712]{1,0:T(8,128)(2,1)S(1)}, u32[]{:S(2)}, u32[]{:S(2)}) %collective-permute-start.10) | collective-permute-done | bytes 118816 | tf_op jit(solution)/shard_map/ppermute | solution.py:194
  19.0 1.6 %collective-permute-start.2 = (bf16[32,3712]{1,0:T(8,128)(2,1)S(1)}, bf16[32,3712]{1,0:T(8,128)(2,1)S(1)}, u32[]{:S(2)}, u32[]{:S(2)}) collective-permute-start(bf16[32,3712]{1,0:T(8,128)(2,1)S(1)} %pad_maximum_fusion), channel_id=1, source_target_pairs={{0,4},{1,3},{2,6},{3,1},{4,0},{5,7},{6,2},{7,5},{8,12},{9,11},{10,... | collective-permute-start | bytes 712712 | tf_op jit(solution)/shard_map/ppermute | solution.py:194
  20.6 2.5 %collective-permute-done.11.refs_1_ = bf16[16,3712]{1,0:T(8,128)(2,1)S(1)} collective-permute-done((bf16[16,3712]{1,0:T(8,128)(2,1)S(1)}, bf16[16,3712]{1,0:T(8,128)(2,1)S(1)}, u32[]{:S(2)}, u32[]{:S(2)}) %collective-permute-start.11) | collective-permute-done | bytes 118816 | tf_op jit(solution)/shard_map/ppermute | solution.py:194
  23.1 1.6 %collective-permute-start.12 = (bf16[32,3712]{1,0:T(8,128)(2,1)S(1)}, bf16[32,3712]{1,0:T(8,128)(2,1)S(1)}, u32[]{:S(2)}, u32[]{:S(2)}) collective-permute-start(bf16[32,3712]{1,0:T(8,128)(2,1)S(1)} %pad_maximum_fusion.1), channel_id=1, source_target_pairs={{0,4},{1,3},{2,6},{3,1},{4,0},{5,7},{6,2},{7,5},{8,12},{9,11},{10,... | collective-permute-start | bytes 712712 | tf_op jit(solution)/shard_map/ppermute | solution.py:194
  25.6 1.6 %collective-permute-start.22 = (bf16[32,3712]{1,0:T(8,128)(2,1)S(1)}, bf16[32,3712]{1,0:T(8,128)(2,1)S(1)}, u32[]{:S(2)}, u32[]{:S(2)}) collective-permute-start(bf16[32,3712]{1,0:T(8,128)(2,1)S(1)} %pad_maximum_fusion.2), channel_id=1, source_target_pairs={{0,4},{1,3},{2,6},{3,1},{4,0},{5,7},{6,2},{7,5},{8,12},{9,11},{10,... | collective-permute-start | bytes 712712 | tf_op jit(solution)/shard_map/ppermute | solution.py:194
  30.1 1.7 %collective-permute-done.22.refs_2_ = bf16[32,3712]{1,0:T(8,128)(2,1)S(1)} collective-permute-done((bf16[32,3712]{1,0:T(8,128)(2,1)S(1)}, bf16[32,3712]{1,0:T(8,128)(2,1)S(1)}, u32[]{:S(2)}, u32[]{:S(2)}) %collective-permute-start.22) | collective-permute-done | bytes 237600 | tf_op jit(solution)/shard_map/ppermute | solution.py:194
  32.3 2.0 %copy-done = bf16[1,3584,512]{2,1,0:T(8,128)(2,1)S(1)} copy-done((bf16[1,3584,512]{2,1,0:T(8,128)(2,1)S(1)}, bf16[1,3584,512]{2,1,0:T(8,128)(2,1)}, u32[]{:S(2)}) %copy-start) | copy-done | bytes 3670040
  34.4 2.0 %copy-done.2 = bf16[1,3584,512]{2,1,0:T(8,128)(2,1)S(1)} copy-done((bf16[1,3584,512]{2,1,0:T(8,128)(2,1)S(1)}, bf16[1,3584,512]{2,1,0:T(8,128)(2,1)}, u32[]{:S(2)}) %copy-start.2) | copy-done | bytes 3670040
  36.4 2.0 %copy-done.4 = bf16[1,512,3584]{2,1,0:T(8,128)(2,1)S(1)} copy-done((bf16[1,512,3584]{2,1,0:T(8,128)(2,1)S(1)}, bf16[1,512,3584]{2,1,0:T(8,128)(2,1)}, u32[]{:S(2)}) %copy-start.4) | copy-done | bytes 3670040
  38.4 2.4 %ffn_3.1 = (bf16[64,3584]{1,0:T(8,128)(2,1)S(1)}, bf16[64,3584]{1,0:T(8,128)(2,1)S(1)}) custom-call(s32[2]{0:T(128)S(1)} %pad_add_fusion.index_ref, bf16[16,3712]{1,0:T(8,128)(2,1)S(1)} %collective-permute-done.refs_0_, bf16[16,3712]{1,0:T(8,128)(2,1)S(1)} %collective-permute-done.1.refs_1_, bf16[32,3712]{1,0:T(8,128)(2,1)S(1)} %collective-permute-done.2.refs_2_, ...), custom_call_target="tpu_custom_call" | custom-call | flops 1409286144 | bytes 1835008 | tf_op jit(solution)/shard_map/ffn_3/pallas_call | solution.py:98
  42.7 2.4 %ffn_2.1 = (bf16[64,3584]{1,0:T(8,128)(2,1)S(1)}, bf16[64,3584]{1,0:T(8,128)(2,1)S(1)}) custom-call(s32[2]{0:T(128)S(1)} %pad_add_fusion.index_ref, bf16[16,3712]{1,0:T(8,128)(2,1)S(1)} %collective-permute-done.10.refs_0_, bf16[16,3712]{1,0:T(8,128)(2,1)S(1)} %collective-permute-done.11.refs_1_, bf16[32,3712]{1,0:T(8,128)(2,1)S(1)} %collective-permute-done.12.refs_2_, ...), custom_call_target="tpu_custom_call" | custom-call | flops 1409286144 | bytes 1835008 | tf_op jit(solution)/shard_map/ffn_2/pallas_call | solution.py:98
  45.8 2.4 %ffn_1.1 = (bf16[64,3584]{1,0:T(8,128)(2,1)S(1)}, bf16[64,3584]{1,0:T(8,128)(2,1)S(1)}) custom-call(s32[2]{0:T(128)S(1)} %pad_add_fusion.index_ref, bf16[16,3712]{1,0:T(8,128)(2,1)S(1)} %collective-permute-done.20.refs_0_, bf16[16,3712]{1,0:T(8,128)(2,1)S(1)} %collective-permute-done.21.refs_1_, bf16[32,3712]{1,0:T(8,128)(2,1)S(1)} %collective-permute-done.22.refs_2_, ...), custom_call_target="tpu_custom_call" | custom-call | flops 1409286144 | bytes 1835008 | tf_op jit(solution)/shard_map/ffn_1/pallas_call | solution.py:98
  49.9 3.7 %ffn_0.1 = (bf16[64,3584]{1,0:T(8,128)(2,1)S(1)}, bf16[64,3584]{1,0:T(8,128)(2,1)S(1)}) custom-call(s32[2]{0:T(128)S(1)} %pad_add_fusion.index_ref, bf16[16,3712]{1,0:T(8,128)(2,1)S(1)} %copy-done.9, bf16[16,3712]{1,0:T(8,128)(2,1)S(1)} %collective-permute-done.30.refs_1_, bf16[32,3712]{1,0:T(8,128)(2,1)S(1)} %collective-permute-done.31.refs_2_, ...), custom_call_target="tpu_custom_call" | custom-call | flops 2818572288 | bytes 1835008 | tf_op jit(solution)/shard_map/ffn_0/pallas_call | solution.py:98
  58.3 1.6 %collective-permute-done.7.refs_2_ = bf16[32,3584]{1,0:T(8,128)(2,1)S(1)} collective-permute-done((bf16[32,3584]{1,0:T(8,128)(2,1)S(1)}, bf16[32,3584]{1,0:T(8,128)(2,1)S(1)}, u32[]{:S(2)}, u32[]{:S(2)}) %collective-permute-start.7) | collective-permute-done | bytes 229408 | tf_op jit(solution)/shard_map/ppermute | solution.py:197
  64.1 3.2 %collective-permute-done.27.refs_2_ = bf16[32,3584]{1,0:T(8,128)(2,1)S(1)} collective-permute-done((bf16[32,3584]{1,0:T(8,128)(2,1)S(1)}, bf16[32,3584]{1,0:T(8,128)(2,1)S(1)}, u32[]{:S(2)}, u32[]{:S(2)}) %collective-permute-start.27) | collective-permute-done | bytes 229408 | tf_op jit(solution)/shard_map/ppermute | solution.py:197
  68.9 2.1 %collective-permute-done.36.refs_2_ = bf16[32,3584]{1,0:T(8,128)(2,1)S(1)} collective-permute-done((bf16[32,3584]{1,0:T(8,128)(2,1)S(1)}, bf16[32,3584]{1,0:T(8,128)(2,1)S(1)}, u32[]{:S(2)}, u32[]{:S(2)}) %collective-permute-start.36) | collective-permute-done | bytes 229408 | tf_op jit(solution)/shard_map/ppermute | solution.py:197
  72.6 2.5 %collective-permute-start.9 = (bf16[16,3584]{1,0:T(8,128)(2,1)S(1)}, bf16[16,3584]{1,0:T(8,128)(2,1)S(1)}, u32[]{:S(2)}, u32[]{:S(2)}) collective-permute-start(bf16[16,3584]{1,0:T(8,128)(2,1)S(1)} %sum_far.4), channel_id=1, source_target_pairs={{24,0},{25,1},{26,2},{27,3},{28,4},{29,5},{30,6},{31,7},{16,8},{17... | collective-permute-start | bytes 344072 | tf_op jit(solution)/shard_map/ppermute | solution.py:197
  75.3 2.0 %collective-permute-start.29 = (bf16[16,3584]{1,0:T(8,128)(2,1)S(1)}, bf16[16,3584]{1,0:T(8,128)(2,1)S(1)}, u32[]{:S(2)}, u32[]{:S(2)}) collective-permute-start(bf16[16,3584]{1,0:T(8,128)(2,1)S(1)} %sum_far.6), channel_id=1, source_target_pairs={{8,0},{9,1},{10,2},{11,3},{12,4},{13,5},{14,6},{15,7},{0,8},{1,9},... | collective-permute-start | bytes 344072 | tf_op jit(solution)/shard_map/ppermute | solution.py:197
  77.4 3.1 %collective-permute-done.9.refs_0_ = bf16[16,3584]{1,0:T(8,128)(2,1)S(1)} collective-permute-done((bf16[16,3584]{1,0:T(8,128)(2,1)S(1)}, bf16[16,3584]{1,0:T(8,128)(2,1)S(1)}, u32[]{:S(2)}, u32[]{:S(2)}) %collective-permute-start.9) | collective-permute-done | bytes 114720 | tf_op jit(solution)/shard_map/ppermute | solution.py:197
  80.5 3.9 %collective-permute-done.19.refs_1_ = bf16[16,3584]{1,0:T(8,128)(2,1)S(1)} collective-permute-done((bf16[16,3584]{1,0:T(8,128)(2,1)S(1)}, bf16[16,3584]{1,0:T(8,128)(2,1)S(1)}, u32[]{:S(2)}, u32[]{:S(2)}) %collective-permute-start.19) | collective-permute-done | bytes 114720 | tf_op jit(solution)/shard_map/ppermute | solution.py:197
  (95 shorter events, 24.6 us)
Async XLA Ops:
  1.7 9.4 %collective-permute-start = (bf16[16,3712]{1,0:T(8,128)(2,1)}, bf16[16,3712]{1,0:T(8,128)(2,1)S(1)}, u32[]{:S(2)}, u32[]{:S(2)}) collective-permute-start(bf16[16,3712]{1,0:T(8,128)(2,1)} %pack.1.refs_0_), channel_id=1, source_target_pairs={{0,24},{1,25},{2,26},{3,27},{4,28},{5,29},{6,30},{7,31},{8,16},{9,... | collective-permute-start | bytes 356360 | tf_op jit(solution)/shard_map/ppermute | solution.py:194
  6.7 10.2 %collective-permute-start.10 = (bf16[16,3712]{1,0:T(8,128)(2,1)}, bf16[16,3712]{1,0:T(8,128)(2,1)S(1)}, u32[]{:S(2)}, u32[]{:S(2)}) collective-permute-start(bf16[16,3712]{1,0:T(8,128)(2,1)} %pack.1.refs_0_), channel_id=1, source_target_pairs={{0,16},{1,17},{2,18},{3,19},{4,20},{5,21},{6,22},{7,23},{8,24},{9,... | collective-permute-start | bytes 356360 | tf_op jit(solution)/shard_map/ppermute | solution.py:194
  6.7 11.7 %collective-permute-start.20 = (bf16[16,3712]{1,0:T(8,128)(2,1)}, bf16[16,3712]{1,0:T(8,128)(2,1)S(1)}, u32[]{:S(2)}, u32[]{:S(2)}) collective-permute-start(bf16[16,3712]{1,0:T(8,128)(2,1)} %pack.1.refs_0_), channel_id=1, source_target_pairs={{0,8},{1,9},{2,10},{3,11},{4,12},{5,13},{6,14},{7,15},{8,0},{9,1},... | collective-permute-start | bytes 356360 | tf_op jit(solution)/shard_map/ppermute | solution.py:194
  11.1 7.9 %collective-permute-start.1 = (bf16[16,3712]{1,0:T(8,128)(2,1)S(1)}, bf16[16,3712]{1,0:T(8,128)(2,1)S(1)}, u32[]{:S(2)}, u32[]{:S(2)}) collective-permute-start(bf16[16,3712]{1,0:T(8,128)(2,1)S(1)} %collective-permute-done.refs_0_), channel_id=1, source_target_pairs={{0,2},{1,5},{2,0},{3,7},{4,6},{5,1},{6,4},{7,3},{8,10},{9,13},{10,... | collective-permute-start | bytes 356360 | tf_op jit(solution)/shard_map/ppermute | solution.py:194
  12.8 14.4 %collective-permute-start.30 = (bf16[16,3712]{1,0:T(8,128)(2,1)}, bf16[16,3712]{1,0:T(8,128)(2,1)S(1)}, u32[]{:S(2)}, u32[]{:S(2)}) collective-permute-start(bf16[16,3712]{1,0:T(8,128)(2,1)} %pack.1.refs_0_), channel_id=1, source_target_pairs={{0,2},{1,5},{2,0},{3,7},{4,6},{5,1},{6,4},{7,3},{8,10},{9,13},{10,... | collective-permute-start | bytes 356360 | tf_op jit(solution)/shard_map/ppermute | solution.py:194
  13.1 15.5 %collective-permute-start.3 = (bf16[16,3712]{1,0:T(8,128)(2,1)S(1)}, bf16[16,3712]{1,0:T(8,128)(2,1)S(1)}, u32[]{:S(2)}, u32[]{:S(2)}) collective-permute-start(bf16[16,3712]{1,0:T(8,128)(2,1)S(1)} %collective-permute-done.refs_0_), channel_id=1, source_target_pairs={{0,1},{1,0},{2,3},{3,2},{4,5},{5,4},{6,7},{7,6},{8,9},{9,8},{10,11... | collective-permute-start | bytes 356360 | tf_op jit(solution)/shard_map/ppermute | solution.py:194
  19.0 8.2 %collective-permute-start.2 = (bf16[32,3712]{1,0:T(8,128)(2,1)S(1)}, bf16[32,3712]{1,0:T(8,128)(2,1)S(1)}, u32[]{:S(2)}, u32[]{:S(2)}) collective-permute-start(bf16[32,3712]{1,0:T(8,128)(2,1)S(1)} %pad_maximum_fusion), channel_id=1, source_target_pairs={{0,4},{1,3},{2,6},{3,1},{4,0},{5,7},{6,2},{7,5},{8,12},{9,11},{10,... | collective-permute-start | bytes 712712 | tf_op jit(solution)/shard_map/ppermute | solution.py:194
  28.7 12.8 %collective-permute-start.31 = (bf16[32,3712]{1,0:T(8,128)(2,1)S(1)}, bf16[32,3712]{1,0:T(8,128)(2,1)S(1)}, u32[]{:S(2)}, u32[]{:S(2)}) collective-permute-start(bf16[32,3712]{1,0:T(8,128)(2,1)S(1)} %pad_maximum_fusion.3), channel_id=1, source_target_pairs={{0,4},{1,3},{2,6},{3,1},{4,0},{5,7},{6,2},{7,5},{8,12},{9,11},{10,... | collective-permute-start | bytes 712712 | tf_op jit(solution)/shard_map/ppermute | solution.py:194
  29.3 12.2 %collective-permute-start.15 = (bf16[32,3712]{1,0:T(8,128)(2,1)S(1)}, bf16[32,3712]{1,0:T(8,128)(2,1)S(1)}, u32[]{:S(2)}, u32[]{:S(2)}) collective-permute-start(bf16[32,3712]{1,0:T(8,128)(2,1)S(1)} %collective-permute-done.12.refs_2_), channel_id=1, source_target_pairs={{0,1},{1,0},{2,3},{3,2},{4,5},{5,4},{6,7},{7,6},{8,9},{9,8},{10,11... | collective-permute-start | bytes 712712 | tf_op jit(solution)/shard_map/ppermute | solution.py:194
  30.1 10.7 %collective-permute-start.13 = (bf16[16,3712]{1,0:T(8,128)(2,1)S(1)}, bf16[16,3712]{1,0:T(8,128)(2,1)S(1)}, u32[]{:S(2)}, u32[]{:S(2)}) collective-permute-start(bf16[16,3712]{1,0:T(8,128)(2,1)S(1)} %collective-permute-done.10.refs_0_), channel_id=1, source_target_pairs={{0,1},{1,0},{2,3},{3,2},{4,5},{5,4},{6,7},{7,6},{8,9},{9,8},{10,11... | collective-permute-start | bytes 356360 | tf_op jit(solution)/shard_map/ppermute | solution.py:194
  31.8 9.1 %collective-permute-start.14 = (bf16[16,3712]{1,0:T(8,128)(2,1)S(1)}, bf16[16,3712]{1,0:T(8,128)(2,1)S(1)}, u32[]{:S(2)}, u32[]{:S(2)}) collective-permute-start(bf16[16,3712]{1,0:T(8,128)(2,1)S(1)} %collective-permute-done.11.refs_1_), channel_id=1, source_target_pairs={{0,1},{1,0},{2,3},{3,2},{4,5},{5,4},{6,7},{7,6},{8,9},{9,8},{10,11... | collective-permute-start | bytes 356360 | tf_op jit(solution)/shard_map/ppermute | solution.py:194
  31.8 13.9 %collective-permute-start.25 = (bf16[32,3712]{1,0:T(8,128)(2,1)S(1)}, bf16[32,3712]{1,0:T(8,128)(2,1)S(1)}, u32[]{:S(2)}, u32[]{:S(2)}) collective-permute-start(bf16[32,3712]{1,0:T(8,128)(2,1)S(1)} %collective-permute-done.22.refs_2_), channel_id=1, source_target_pairs={{0,1},{1,0},{2,3},{3,2},{4,5},{5,4},{6,7},{7,6},{8,9},{9,8},{10,11... | collective-permute-start | bytes 712712 | tf_op jit(solution)/shard_map/ppermute | solution.py:194
  40.8 7.4 %collective-permute-start.32 = (bf16[16,3712]{1,0:T(8,128)(2,1)S(1)}, bf16[16,3712]{1,0:T(8,128)(2,1)S(1)}, u32[]{:S(2)}, u32[]{:S(2)}) collective-permute-start(bf16[16,3712]{1,0:T(8,128)(2,1)S(1)} %copy-done.9), channel_id=1, source_target_pairs={{0,1},{1,0},{2,3},{3,2},{4,5},{5,4},{6,7},{7,6},{8,9},{9,8},{10,11... | collective-permute-start | bytes 356360 | tf_op jit(solution)/shard_map/ppermute | solution.py:194
  45.2 8.6 %collective-permute-start.6 = (bf16[64,3584]{1,0:T(8,128)(2,1)S(1)}, bf16[64,3584]{1,0:T(8,128)(2,1)S(1)}, u32[]{:S(2)}, u32[]{:S(2)}) collective-permute-start(bf16[64,3584]{1,0:T(8,128)(2,1)S(1)} %get-tuple-element.14), channel_id=1, source_target_pairs={{0,1},{1,0},{2,3},{3,2},{4,5},{5,4},{6,7},{7,6},{8,9},{9,8},{10,11... | collective-permute-start | bytes 1376264 | tf_op jit(solution)/shard_map/ppermute | solution.py:194
  45.7 9.7 %collective-permute-start.16 = (bf16[64,3584]{1,0:T(8,128)(2,1)S(1)}, bf16[64,3584]{1,0:T(8,128)(2,1)S(1)}, u32[]{:S(2)}, u32[]{:S(2)}) collective-permute-start(bf16[64,3584]{1,0:T(8,128)(2,1)S(1)} %get-tuple-element.16), channel_id=1, source_target_pairs={{0,1},{1,0},{2,3},{3,2},{4,5},{5,4},{6,7},{7,6},{8,9},{9,8},{10,11... | collective-permute-start | bytes 1376264 | tf_op jit(solution)/shard_map/ppermute | solution.py:194
  48.2 7.8 %collective-permute-start.26 = (bf16[64,3584]{1,0:T(8,128)(2,1)S(1)}, bf16[64,3584]{1,0:T(8,128)(2,1)S(1)}, u32[]{:S(2)}, u32[]{:S(2)}) collective-permute-start(bf16[64,3584]{1,0:T(8,128)(2,1)S(1)} %get-tuple-element.18), channel_id=1, source_target_pairs={{0,1},{1,0},{2,3},{3,2},{4,5},{5,4},{6,7},{7,6},{8,9},{9,8},{10,11... | collective-permute-start | bytes 1376264 | tf_op jit(solution)/shard_map/ppermute | solution.py:194
  56.1 11.2 %collective-permute-start.27 = (bf16[32,3584]{1,0:T(8,128)(2,1)S(1)}, bf16[32,3584]{1,0:T(8,128)(2,1)S(1)}, u32[]{:S(2)}, u32[]{:S(2)}) collective-permute-start(bf16[32,3584]{1,0:T(8,128)(2,1)S(1)} %sum_second.6), channel_id=1, source_target_pairs={{4,0},{3,1},{6,2},{1,3},{0,4},{7,5},{2,6},{5,7},{12,8},{11,9},{14,... | collective-permute-start | bytes 688136 | tf_op jit(solution)/shard_map/ppermute | solution.py:197
  57.7 13.2 %collective-permute-start.36 = (bf16[32,3584]{1,0:T(8,128)(2,1)S(1)}, bf16[32,3584]{1,0:T(8,128)(2,1)S(1)}, u32[]{:S(2)}, u32[]{:S(2)}) collective-permute-start(bf16[32,3584]{1,0:T(8,128)(2,1)S(1)} %sum_second.7), channel_id=1, source_target_pairs={{4,0},{3,1},{6,2},{1,3},{0,4},{7,5},{2,6},{5,7},{12,8},{11,9},{14,... | collective-permute-start | bytes 688136 | tf_op jit(solution)/shard_map/ppermute | solution.py:197
  60.0 12.6 %collective-permute-start.8 = (bf16[16,3584]{1,0:T(8,128)(2,1)S(1)}, bf16[16,3584]{1,0:T(8,128)(2,1)S(1)}, u32[]{:S(2)}, u32[]{:S(2)}) collective-permute-start(bf16[16,3584]{1,0:T(8,128)(2,1)S(1)} %sum_first.4), channel_id=1, source_target_pairs={{2,0},{5,1},{0,2},{7,3},{6,4},{1,5},{4,6},{3,7},{10,8},{13,9},{8,1... | collective-permute-start | bytes 344072 | tf_op jit(solution)/shard_map/ppermute | solution.py:197
  62.5 12.6 %collective-permute-start.18 = (bf16[16,3584]{1,0:T(8,128)(2,1)S(1)}, bf16[16,3584]{1,0:T(8,128)(2,1)S(1)}, u32[]{:S(2)}, u32[]{:S(2)}) collective-permute-start(bf16[16,3584]{1,0:T(8,128)(2,1)S(1)} %sum_first.5), channel_id=1, source_target_pairs={{2,0},{5,1},{0,2},{7,3},{6,4},{1,5},{4,6},{3,7},{10,8},{13,9},{8,1... | collective-permute-start | bytes 344072 | tf_op jit(solution)/shard_map/ppermute | solution.py:197
  67.3 7.9 %collective-permute-start.28 = (bf16[16,3584]{1,0:T(8,128)(2,1)S(1)}, bf16[16,3584]{1,0:T(8,128)(2,1)S(1)}, u32[]{:S(2)}, u32[]{:S(2)}) collective-permute-start(bf16[16,3584]{1,0:T(8,128)(2,1)S(1)} %sum_first.6), channel_id=1, source_target_pairs={{2,0},{5,1},{0,2},{7,3},{6,4},{1,5},{4,6},{3,7},{10,8},{13,9},{8,1... | collective-permute-start | bytes 344072 | tf_op jit(solution)/shard_map/ppermute | solution.py:197
  72.6 7.9 %collective-permute-start.9 = (bf16[16,3584]{1,0:T(8,128)(2,1)S(1)}, bf16[16,3584]{1,0:T(8,128)(2,1)S(1)}, u32[]{:S(2)}, u32[]{:S(2)}) collective-permute-start(bf16[16,3584]{1,0:T(8,128)(2,1)S(1)} %sum_far.4), channel_id=1, source_target_pairs={{24,0},{25,1},{26,2},{27,3},{28,4},{29,5},{30,6},{31,7},{16,8},{17... | collective-permute-start | bytes 344072 | tf_op jit(solution)/shard_map/ppermute | solution.py:197
  75.2 9.3 %collective-permute-start.19 = (bf16[16,3584]{1,0:T(8,128)(2,1)S(1)}, bf16[16,3584]{1,0:T(8,128)(2,1)S(1)}, u32[]{:S(2)}, u32[]{:S(2)}) collective-permute-start(bf16[16,3584]{1,0:T(8,128)(2,1)S(1)} %sum_far.5), channel_id=1, source_target_pairs={{16,0},{17,1},{18,2},{19,3},{20,4},{21,5},{22,6},{23,7},{24,8},{25... | collective-permute-start | bytes 344072 | tf_op jit(solution)/shard_map/ppermute | solution.py:197
  75.3 9.1 %collective-permute-start.29 = (bf16[16,3584]{1,0:T(8,128)(2,1)S(1)}, bf16[16,3584]{1,0:T(8,128)(2,1)S(1)}, u32[]{:S(2)}, u32[]{:S(2)}) collective-permute-start(bf16[16,3584]{1,0:T(8,128)(2,1)S(1)} %sum_far.6), channel_id=1, source_target_pairs={{8,0},{9,1},{10,2},{11,3},{12,4},{13,5},{14,6},{15,7},{0,8},{1,9},... | collective-permute-start | bytes 344072 | tf_op jit(solution)/shard_map/ppermute | solution.py:197
  (24 other events, 105.4 us)

commit v3 on v2

--- a/solution.py
+++ b/solution.py
@@ -49,58 +49,94 @@
     )(tokens, expert_ids.T, route_weight.T)
 
 
-def ffn_body(n_parts, with_shared, share_of, index_ref, *refs):
+def ffn_body(n_parts, n_weights, fresh, share_of, index_ref, *refs):
     parts, refs = refs[: 2 * n_parts], refs[2 * n_parts :]
-    wg_ref, wu_ref, wd_ref = refs[:3]
-    if with_shared:
-        sg_ref, su_ref, sd_ref = refs[3:6]
-    oa_ref, ob_ref, x_ref = refs[-3:]
+    weights, refs = refs[:n_weights], refs[n_weights:]
+    oa_ref, ob_ref = refs[:2]
+    kept, x_ref = refs[2:5], refs[5]
     rows, model = oa_ref.shape
+    steps = split_of(model)
+    tile = model // steps
+    copies = []
+    if fresh:
+        sems = refs[6]
+        for i in range(steps):
+            at = pl.ds(i * tile, tile)
+            for n in (0, 1):
+                copies.append(
+                    pltpu.make_async_copy(weights[n].at[at], kept[n].at[at], sems.at[n, i])
+                )
+        size = weights[2].shape[0] // steps
+        for i in range(steps):
+            at = pl.ds(i * size, size)
+            copies.append(pltpu.make_async_copy(weights[2].at[at], kept[2].at[at], sems.at[2, i]))
+        for copy in copies:
+            copy.start()
+        weights = kept
     start = 0
     for part in parts:
         x_ref[start : start + part.shape[0], :] = part[...]
         start += part.shape[0]
-    x = x_ref[:, :model]
-
-    def hidden(g_ref, u_ref):
-        g = jnp.dot(x, g_ref[...], preferred_element_type=jnp.float32)
-        u = jnp.dot(x, u_ref[...], preferred_element_type=jnp.float32)
+
+    def hidden(g_ref, u_ref, waits=()):
+        if not waits:
+            x = x_ref[:, :model]
+            g = jnp.dot(x, g_ref[...], preferred_element_type=jnp.float32)
+            u = jnp.dot(x, u_ref[...], preferred_element_type=jnp.float32)
+        else:
+            g = u = jnp.zeros((2 * rows, g_ref.shape[1]), jnp.float32)
+            for i in range(steps):
+                at = slice(i * tile, (i + 1) * tile)
+                for copy in waits[2 * i : 2 * i + 2]:
+                    copy.wait()
+                x = x_ref[:, at]
+                g = g + jnp.dot(x, g_ref[at, :], preferred_element_type=jnp.float32)
+                u = u + jnp.dot(x, u_ref[at, :], preferred_element_type=jnp.float32)
         return (jax.nn.silu(g) * u).astype(jnp.bfloat16)
 
-    h = hidden(wg_ref, wu_ref)
+    h = hidden(weights[0], weights[1], copies[: 2 * steps])
     width = x_ref.shape[1] - model
     lane = lax.broadcasted_iota(jnp.int32, (2 * rows, width), 1)
     mine = (lane == index_ref[0]) | (lane == index_ref[0] + width // 2)
     code = x_ref[:, model:].astype(jnp.float32)
     scale = jnp.sum(jnp.where(mine, code, 0.0), axis=1, keepdims=True)
-    if with_shared:
-        s = hidden(sg_ref, su_ref)
+    if n_weights > 3:
+        s = hidden(weights[3], weights[4])
         row = lax.broadcasted_iota(jnp.int32, (2 * rows, 1), 0)
         share = share_of(row, rows, index_ref[1])
-    steps = split_of(model)
-    tile = model // steps
+    for copy in copies[2 * steps :]:
+        copy.wait()
     for i in range(steps):
         at = slice(i * tile, (i + 1) * tile)
-        y = jnp.dot(h, wd_ref[:, at], preferred_element_type=jnp.float32) * scale
-        if with_shared:
-            more = jnp.dot(s, sd_ref[:, at], preferred_element_type=jnp.float32)
+        y = jnp.dot(h, weights[2][:, at], preferred_element_type=jnp.float32) * scale
+        if n_weights > 3:
+            more = jnp.dot(s, weights[5][:, at], preferred_element_type=jnp.float32)
             y = y + jnp.where(share, more, 0.0)
         oa_ref[:, at] = y[:rows].astype(oa_ref.dtype)
         ob_ref[:, at] = y[rows:].astype(ob_ref.dtype)
 
 
-def ffn(own_parts, other_parts, index, weights, share_of, name):
+def ffn(own_parts, other_parts, index, weights, fresh, share_of, name):
     rows = sum(p.shape[0] for p in own_parts)
     wide = own_parts[0].shape[1]
     hid, model = weights[2].shape
     out = jax.ShapeDtypeStruct((rows, model), jnp.bfloat16)
     parts = [*own_parts, *other_parts]
+    held = 0 if fresh else 3
+    spaces = [pltpu.HBM if fresh else pltpu.VMEM] * 3 + [pltpu.VMEM] * (len(weights) - 3)
+    weights = [pltpu.with_memory_space_constraint(w, s) for w, s in zip(weights, spaces)]
+    scratch = [pltpu.VMEM((2 * rows, wide), jnp.bfloat16)]
+    if fresh:
+        scratch.append(pltpu.SemaphoreType.DMA((3, split_of(model))))
     return pl.pallas_call(
-        functools.partial(ffn_body, len(own_parts), len(weights) > 3, share_of),
-        out_shape=(out, out),
-        in_specs=[pl.BlockSpec(memory_space=pltpu.SMEM)] + [IN_VMEM] * (len(parts) + len(weights)),
-        out_specs=(IN_VMEM, IN_VMEM),
-        scratch_shapes=[pltpu.VMEM((2 * rows, wide), jnp.bfloat16)],
+        functools.partial(ffn_body, len(own_parts), len(weights), fresh, share_of),
+        out_shape=(out, out, *[pltpu.VMEM(w.shape, w.dtype) for w in weights[:3]]),
+        in_specs=[pl.BlockSpec(memory_space=pltpu.SMEM)]
+        + [IN_VMEM] * len(parts)
+        + [pl.BlockSpec(memory_space=s) for s in spaces],
+        out_specs=(IN_VMEM,) * 5,
+        input_output_aliases={1 + len(parts) + i: 2 + i for i in range(held)},
+        scratch_shapes=scratch,
         compiler_params=params(),
         cost_estimate=pl.CostEstimate(
             flops=4 * rows * model * hid * len(weights),
@@ -210,9 +246,8 @@
 
     core = lax.axis_index("pair")
     index = jnp.stack([lax.axis_index("expert") * n_pair + core, core]).astype(jnp.int32)
-    pin = lambda w: pltpu.with_memory_space_constraint(w, pltpu.VMEM)
-    routed_weights = [pin(w.reshape(w.shape[-2:])) for w in (w_gate, w_up, w_down)]
-    shared_weights = [pin(w) for w in (s_gate, s_up, s_down)]
+    weights = [w.reshape(w.shape[-2:]) for w in (w_gate, w_up, w_down)]
+    shared = [s_gate, s_up, s_down]
     width = -(-2 * n_expert * n_pair // LANES) * LANES
     block = pack(tokens, expert_ids, route_weight, width)
 
@@ -227,35 +262,78 @@
 
     order = list(range(far - 1, -1, -1))
     far_route = {k: routes.along_far(k) for k in range(1, far)}
-    mine, theirs, head = {}, {}, {}
+    many = len(first) + 1
+    head, parts, others, pair, out = {}, {}, {}, {}, {}
     for k in order:
         head[k] = routes.send(block, far_route[k]) if k else block
     for k in order:
-        parts = [head[k]] + [routes.send(head[k], r) for r in first]
+        parts[k] = [head[k]] + [routes.send(head[k], r) for r in first]
         if second is not None:
-            parts.append(routes.send(jnp.concatenate(parts, axis=0), second))
-        others = [routes.send(p, cross) for p in parts]
-        weights = routed_weights + (shared_weights if k == 0 else [])
-        mine[k], other = ffn(parts, others, index, weights, share_of, "ffn_%d" % k)
-        theirs[k] = routes.send(other, cross)
-
+            parts[k].append(routes.send(jnp.concatenate(parts[k], axis=0), second))
+        others[k] = [routes.send(p, cross) for p in parts[k]]
+
+    came = {k: [] for k in order}
+    home = {k: [] for k in order}
     last = []
-    for k in order:
-        pair = [mine[k], theirs[k]]
-        many = len(first) + 1
-        terms = lambda start, more: [(a, start) for a in pair] + more
-        came = []
+
+    def compute(k):
+        given = [*weights, *(shared if k == 0 else [])]
+        fresh = k == order[0]
+        mine, other, *kept = ffn(parts[k], others[k], index, given, fresh, share_of, "ffn_%d" % k)
+        weights[:] = kept
+        pair[k] = [mine, routes.send(other, cross)]
+
+    def sum_second(k):
         if second is not None:
-            out = sums(terms(many * rows, []), many * rows, jnp.bfloat16, "sum_second")
-            came = [routes.send_back(out, second)]
-        home = []
-        for j, r in enumerate(first):
-            at = (j + 1) * rows
-            out = sums(terms(at, [(a, at) for a in came]), rows, jnp.bfloat16, "sum_first")
-            home.append(routes.send_back(out, r))
-        dtype = jnp.bfloat16 if k else jnp.float32
-        out = sums(terms(0, [(a, 0) for a in came + home]), rows, dtype, "sum_far")
-        last.append(routes.send_back(out, far_route[k]) if k else out)
+            at = many * rows
+            out[k] = sums([(a, at) for a in pair[k]], at, jnp.bfloat16, "sum_second")
+
+    def send_second(k):
+        if second is not None:
+            came[k] = [routes.send_back(out[k], second)]
+
+    def sum_first(k):
+        out[k] = [
+            sums([(a, j * rows) for a in pair[k] + came[k]], rows, jnp.bfloat16, "sum_first")
+            for j in range(1, many)
+        ]
+
+    def send_first(k):
+        home[k] = [routes.send_back(o, r) for o, r in zip(out[k], first)]
+
+    def sum_far(k):
+        terms = [(a, 0) for a in pair[k] + came[k] + home[k]]
+        out[k] = sums(terms, rows, jnp.bfloat16 if k else jnp.float32, "sum_far")
+
+    def send_far(k):
+        last.append(routes.send_back(out[k], far_route[k]) if k else out[k])
+
+    def tie(a, b):
+        return lax.optimization_barrier((a, b))
+
+    for k in order[:-1]:
+        compute(k)
+        sum_second(k)
+        send_second(k)
+    lead = order[0]
+    sum_first(lead)
+    parts[0][0], out[lead][0] = tie(parts[0][0], out[lead][0])
+    send_first(lead)
+    compute(0)
+    sum_second(0)
+    sum_far(lead)
+    send_far(lead)
+    send_second(0)
+    for k in order[1:-1]:
+        sum_first(k)
+        send_first(k)
+        sum_far(k)
+        send_far(k)
+    sum_first(0)
+    out[0][0], last[0] = tie(out[0][0], last[0])
+    send_first(0)
+    sum_far(0)
+    send_far(0)
     return sums([(a, 0) for a in last], rows, jnp.bfloat16, "sum_last")
 
 

time: 85.4 us -> 76.7 us (0.90)
  local copies, waits for them, and re-layouts: 8.05 us -> 1.16 us
  waiting for transfers between devices: 27.7 us -> 23.4 us
  Pallas kernels: 13.8 us -> 17 us
  other arithmetic: 1.05 us -> 0.17 us
    unnamed x20 -> x8, local copies, waits for them, and re-layouts: 8.05 us -> 1.16 us
    ppermute x11, waiting for transfers between devices: 14.9 us -> 9.3 us  [send_back(): lax.ppermute(x, self.axes, [(to, fro) for fro, to in enumerate(route)])]
    pallas_call x4, Pallas kernels: 10.8 us -> 14 us  [ffn(): pl.pallas_call(functools.partial(ffn_body, len(own_parts), len(weights),...]
    ppermute x27, waiting for transfers between devices: 12.8 us -> 14.1 us  [send(): return lax.ppermute(x, self.axes, list(enumerate(route)))]
    concatenate x4, other arithmetic: 0.98 us -> 0.1 us  [per_device(): parts[k].append(routes.send(jnp.concatenate(parts[k], axis=0), second))]
  transfers between devices with their start and end apart: 38 -> 38, of which waited for: 11 -> 12; matrix products, arithmetic and copies ran while one was open for 1% -> 0% of each run, Pallas kernels for 13% -> 19%
where the time goes in v3:
time: 76.7 us; the launch traced here: 76.5 us
  starting transfers between devices  34.6 us (45%)
  waiting for transfers between devices  23.4 us (31%)
  Pallas kernels  17 us (22%)
  local copies, waits for them, and re-layouts  1.16 us (2%)
    ppermute x27, starting transfers between devices, send(): return lax.ppermute(x, self.axes, list(enumerate(route)))  19.5 us
    ppermute x11, starting transfers between devices, send_back(): lax.ppermute(x, self.axes, [(to, fro) for fro, to in enumerate(route)])  15.1 us
    ppermute x27, waiting for transfers between devices, send(): return lax.ppermute(x, self.axes, list(enumerate(route)))  14.1 us
    pallas_call x4, Pallas kernels, ffn(): pl.pallas_call(functools.partial(ffn_body, len(own_parts), len(weights),...  14 us
    ppermute x11, waiting for transfers between devices, send_back(): lax.ppermute(x, self.axes, [(to, fro) for fro, to in enumerate(route)])  9.3 us
    pallas_call x1, Pallas kernels, pack(): pl.pallas_call(pack_body, out_shape=jax.ShapeDtypeStruct((rows, model + w...  1.66 us
  transfers between devices with their start and end apart: 38, of which 12 were waited for; matrix products, arithmetic and copies ran while one was open for 0% of the time, Pallas kernels for 19%

profile of v3, /device:TPU:0, one launch (start us, length us, event | category | flops | bytes accessed | tf_op | source)
XLA Modules:
  0.0 76.5 jit_solution(9002189073259956900)
XLA Ops:
  0.0 1.7 %pack.1.refs_0_ = bf16[16,3712]{1,0:T(8,128)(2,1)} custom-call(bf16[16,3584]{1,0:T(8,128)(2,1)} %tokens_ref.1, s32[8,16]{1,0:T(8,128)} %bitcast.10, f32[8,16]{1,0:T(8,128)} %bitcast.11), custom_call_target="tpu_custom_call" | custom-call | tf_op jit(solution)/shard_map/pack/pallas_call | solution.py:43
  1.7 5.0 %collective-permute-start = (bf16[16,3712]{1,0:T(8,128)(2,1)}, bf16[16,3712]{1,0:T(8,128)(2,1)S(1)}, u32[]{:S(2)}, u32[]{:S(2)}) collective-permute-start(bf16[16,3712]{1,0:T(8,128)(2,1)} %pack.1.refs_0_), channel_id=1, source_target_pairs={{0,24},{1,25},{2,26},{3,27},{4,28},{5,29},{6,30},{7,31},{8,16},{9,... | collective-permute-start | bytes 356360 | tf_op jit(solution)/shard_map/ppermute | solution.py:230
  7.3 3.8 %collective-permute-done.refs_0_ = bf16[16,3712]{1,0:T(8,128)(2,1)S(1)} collective-permute-done((bf16[16,3712]{1,0:T(8,128)(2,1)}, bf16[16,3712]{1,0:T(8,128)(2,1)S(1)}, u32[]{:S(2)}, u32[]{:S(2)}) %collective-permute-start) | collective-permute-done | bytes 118816 | tf_op jit(solution)/shard_map/ppermute | solution.py:230
  11.1 1.7 %collective-permute-start.1 = (bf16[16,3712]{1,0:T(8,128)(2,1)S(1)}, bf16[16,3712]{1,0:T(8,128)(2,1)S(1)}, u32[]{:S(2)}, u32[]{:S(2)}) collective-permute-start(bf16[16,3712]{1,0:T(8,128)(2,1)S(1)} %collective-permute-done.refs_0_), channel_id=1, source_target_pairs={{0,2},{1,5},{2,0},{3,7},{4,6},{5,1},{6,4},{7,3},{8,10},{9,13},{10,... | collective-permute-start | bytes 356360 | tf_op jit(solution)/shard_map/ppermute | solution.py:230
  13.2 3.7 %collective-permute-done.19.refs_0_ = bf16[16,3712]{1,0:T(8,128)(2,1)S(1)} collective-permute-done((bf16[16,3712]{1,0:T(8,128)(2,1)}, bf16[16,3712]{1,0:T(8,128)(2,1)S(1)}, u32[]{:S(2)}, u32[]{:S(2)}) %collective-permute-start.19) | collective-permute-done | bytes 118816 | tf_op jit(solution)/shard_map/ppermute | solution.py:230
  16.9 1.5 %collective-permute-start.20 = (bf16[16,3712]{1,0:T(8,128)(2,1)S(1)}, bf16[16,3712]{1,0:T(8,128)(2,1)S(1)}, u32[]{:S(2)}, u32[]{:S(2)}) collective-permute-start(bf16[16,3712]{1,0:T(8,128)(2,1)S(1)} %collective-permute-done.19.refs_0_), channel_id=1, source_target_pairs={{0,2},{1,5},{2,0},{3,7},{4,6},{5,1},{6,4},{7,3},{8,10},{9,13},{10,... | collective-permute-start | bytes 356360 | tf_op jit(solution)/shard_map/ppermute | solution.py:230
  19.0 1.6 %collective-permute-start.2 = (bf16[32,3712]{1,0:T(8,128)(2,1)S(1)}, bf16[32,3712]{1,0:T(8,128)(2,1)S(1)}, u32[]{:S(2)}, u32[]{:S(2)}) collective-permute-start(bf16[32,3712]{1,0:T(8,128)(2,1)S(1)} %pad_maximum_fusion), channel_id=1, source_target_pairs={{0,4},{1,3},{2,6},{3,1},{4,0},{5,7},{6,2},{7,5},{8,12},{9,11},{10,... | collective-permute-start | bytes 712712 | tf_op jit(solution)/shard_map/ppermute | solution.py:230
  20.6 2.5 %collective-permute-done.20.refs_1_ = bf16[16,3712]{1,0:T(8,128)(2,1)S(1)} collective-permute-done((bf16[16,3712]{1,0:T(8,128)(2,1)S(1)}, bf16[16,3712]{1,0:T(8,128)(2,1)S(1)}, u32[]{:S(2)}, u32[]{:S(2)}) %collective-permute-start.20) | collective-permute-done | bytes 118816 | tf_op jit(solution)/shard_map/ppermute | solution.py:230
  23.1 1.6 %collective-permute-start.21 = (bf16[32,3712]{1,0:T(8,128)(2,1)S(1)}, bf16[32,3712]{1,0:T(8,128)(2,1)S(1)}, u32[]{:S(2)}, u32[]{:S(2)}) collective-permute-start(bf16[32,3712]{1,0:T(8,128)(2,1)S(1)} %pad_maximum_fusion.3), channel_id=1, source_target_pairs={{0,4},{1,3},{2,6},{3,1},{4,0},{5,7},{6,2},{7,5},{8,12},{9,11},{10,... | collective-permute-start | bytes 712712 | tf_op jit(solution)/shard_map/ppermute | solution.py:230
  26.1 1.6 %collective-permute-start.15 = (bf16[32,3712]{1,0:T(8,128)(2,1)S(1)}, bf16[32,3712]{1,0:T(8,128)(2,1)S(1)}, u32[]{:S(2)}, u32[]{:S(2)}) collective-permute-start(bf16[32,3712]{1,0:T(8,128)(2,1)S(1)} %pad_maximum_fusion.2), channel_id=1, source_target_pairs={{0,4},{1,3},{2,6},{3,1},{4,0},{5,7},{6,2},{7,5},{8,12},{9,11},{10,... | collective-permute-start | bytes 712712 | tf_op jit(solution)/shard_map/ppermute | solution.py:230
  27.7 5.5 %ffn_3.1 = (bf16[64,3584]{1,0:T(8,128)(2,1)S(1)}, bf16[64,3584]{1,0:T(8,128)(2,1)S(1)}, bf16[3584,512]{1,0:T(8,128)(2,1)S(1)}, bf16[3584,512]{1,0:T(8,128)(2,1)S(1)}, bf16[512,3584]{1,0:T(8,128)(2,1)S(1)}) custom-call(s32[2]{0:T(128)S(1)} %pad_add_fusion.index_ref, bf16[16,3712]{1,0:T(8,128)(2,1)S(1)} %collective-permute-done.refs_0_, ...), custom_call_target="tpu_custom_call" | custom-call | flops 1409286144 | bytes 1835008 | tf_op jit(solution)/shard_map/ffn_3/pallas_call | solution.py:131
  33.4 1.4 %collective-permute-start.9 = (bf16[32,3712]{1,0:T(8,128)(2,1)S(1)}, bf16[32,3712]{1,0:T(8,128)(2,1)S(1)}, u32[]{:S(2)}, u32[]{:S(2)}) collective-permute-start(bf16[32,3712]{1,0:T(8,128)(2,1)S(1)} %pad_maximum_fusion.1), channel_id=1, source_target_pairs={{0,4},{1,3},{2,6},{3,1},{4,0},{5,7},{6,2},{7,5},{8,12},{9,11},{10,... | collective-permute-start | bytes 712712 | tf_op jit(solution)/shard_map/ppermute | solution.py:230
  37.0 2.6 %collective-permute-done.9.refs_2_ = bf16[32,3712]{1,0:T(8,128)(2,1)S(1)} collective-permute-done((bf16[32,3712]{1,0:T(8,128)(2,1)S(1)}, bf16[32,3712]{1,0:T(8,128)(2,1)S(1)}, u32[]{:S(2)}, u32[]{:S(2)}) %collective-permute-start.9) | collective-permute-done | bytes 237600 | tf_op jit(solution)/shard_map/ppermute | solution.py:230
  39.6 1.4 %collective-permute-start.7 = (bf16[32,3584]{1,0:T(8,128)(2,1)S(1)}, bf16[32,3584]{1,0:T(8,128)(2,1)S(1)}, u32[]{:S(2)}, u32[]{:S(2)}) collective-permute-start(bf16[32,3584]{1,0:T(8,128)(2,1)S(1)} %sum_second.4), channel_id=1, source_target_pairs={{4,0},{3,1},{6,2},{1,3},{0,4},{7,5},{2,6},{5,7},{12,8},{11,9},{14,... | collective-permute-start | bytes 688136 | tf_op jit(solution)/shard_map/ppermute | solution.py:233
  40.9 2.3 %ffn_2.1 = (bf16[64,3584]{1,0:T(8,128)(2,1)S(1)}, bf16[64,3584]{1,0:T(8,128)(2,1)S(1)}, bf16[3584,512]{1,0:T(8,128)(2,1)S(1)}, bf16[3584,512]{1,0:T(8,128)(2,1)S(1)}, bf16[512,3584]{1,0:T(8,128)(2,1)S(1)}) custom-call(s32[2]{0:T(128)S(1)} %pad_add_fusion.index_ref, ...), custom_call_target="tpu_custom_call", output_to_operand_aliasing={{2}: (7, {}), {3}: (8, {}), {4}: (9, {})} | custom-call | flops 1409286144 | bytes 1835008 | tf_op jit(solution)/shard_map/ffn_2/pallas_call | solution.py:131
  43.9 2.4 %ffn_1.1 = (bf16[64,3584]{1,0:T(8,128)(2,1)S(1)}, bf16[64,3584]{1,0:T(8,128)(2,1)S(1)}, bf16[3584,512]{1,0:T(8,128)(2,1)S(1)}, bf16[3584,512]{1,0:T(8,128)(2,1)S(1)}, bf16[512,3584]{1,0:T(8,128)(2,1)S(1)}) custom-call(s32[2]{0:T(128)S(1)} %pad_add_fusion.index_ref, ...), custom_call_target="tpu_custom_call", output_to_operand_aliasing={{2}: (7, {}), {3}: (8, {}), {4}: (9, {})} | custom-call | flops 1409286144 | bytes 1835008 | tf_op jit(solution)/shard_map/ffn_1/pallas_call | solution.py:131
  48.1 3.7 %ffn_0.1 = (bf16[64,3584]{1,0:T(8,128)(2,1)S(1)}, bf16[64,3584]{1,0:T(8,128)(2,1)S(1)}, bf16[3584,512]{1,0:T(8,128)(2,1)S(1)}, bf16[3584,512]{1,0:T(8,128)(2,1)S(1)}, bf16[512,3584]{1,0:T(8,128)(2,1)S(1)}) custom-call(s32[2]{0:T(128)S(1)} %pad_add_fusion.index_ref, ...), custom_call_target="tpu_custom_call", output_to_operand_aliasing={{2}: (7, {}), {3}: (8, {}), {4}: (9, {})} | custom-call | flops 2818572288 | bytes 1835008 | tf_op jit(solution)/shard_map/ffn_0/pallas_call | solution.py:131
  52.3 1.4 %collective-permute-start.34 = (bf16[32,3584]{1,0:T(8,128)(2,1)S(1)}, bf16[32,3584]{1,0:T(8,128)(2,1)S(1)}, u32[]{:S(2)}, u32[]{:S(2)}) collective-permute-start(bf16[32,3584]{1,0:T(8,128)(2,1)S(1)} %sum_second.7), channel_id=1, source_target_pairs={{4,0},{3,1},{6,2},{1,3},{0,4},{7,5},{2,6},{5,7},{12,8},{11,9},{14,... | collective-permute-start | bytes 688136 | tf_op jit(solution)/shard_map/ppermute | solution.py:233
  56.5 3.1 %collective-permute-done.34.refs_2_ = bf16[32,3584]{1,0:T(8,128)(2,1)S(1)} collective-permute-done((bf16[32,3584]{1,0:T(8,128)(2,1)S(1)}, bf16[32,3584]{1,0:T(8,128)(2,1)S(1)}, u32[]{:S(2)}, u32[]{:S(2)}) %collective-permute-start.34) | collective-permute-done | bytes 229408 | tf_op jit(solution)/shard_map/ppermute | solution.py:233
  61.0 2.5 %collective-permute-start.28 = (bf16[16,3584]{1,0:T(8,128)(2,1)S(1)}, bf16[16,3584]{1,0:T(8,128)(2,1)S(1)}, u32[]{:S(2)}, u32[]{:S(2)}) collective-permute-start(bf16[16,3584]{1,0:T(8,128)(2,1)S(1)} %sum_far.4), channel_id=1, source_target_pairs={{24,0},{25,1},{26,2},{27,3},{28,4},{29,5},{30,6},{31,7},{16,8},{17... | collective-permute-start | bytes 344072 | tf_op jit(solution)/shard_map/ppermute | solution.py:233
  65.0 1.7 %collective-permute-start.36 = (bf16[16,3584]{1,0:T(8,128)(2,1)S(1)}, bf16[16,3584]{1,0:T(8,128)(2,1)S(1)}, u32[]{:S(2)}, u32[]{:S(2)}) collective-permute-start(bf16[16,3584]{1,0:T(8,128)(2,1)S(1)} %sum_far.6), channel_id=1, source_target_pairs={{8,0},{9,1},{10,2},{11,3},{12,4},{13,5},{14,6},{15,7},{0,8},{1,9},... | collective-permute-start | bytes 344072 | tf_op jit(solution)/shard_map/ppermute | solution.py:233
  68.8 2.1 %collective-permute-start.32 = (bf16[16,3584]{1,0:T(8,128)(2,1)S(1)}, bf16[16,3584]{1,0:T(8,128)(2,1)S(1)}, u32[]{:S(2)}, u32[]{:S(2)}) collective-permute-start(bf16[16,3584]{1,0:T(8,128)(2,1)S(1)} %sum_far.5), channel_id=1, source_target_pairs={{16,0},{17,1},{18,2},{19,3},{20,4},{21,5},{22,6},{23,7},{24,8},{25... | collective-permute-start | bytes 344072 | tf_op jit(solution)/shard_map/ppermute | solution.py:233
  70.9 1.7 %collective-permute-done.37.refs_3_ = bf16[16,3584]{1,0:T(8,128)(2,1)S(1)} collective-permute-done((bf16[16,3584]{1,0:T(8,128)(2,1)S(1)}, bf16[16,3584]{1,0:T(8,128)(2,1)S(1)}, u32[]{:S(2)}, u32[]{:S(2)}) %collective-permute-start.37) | collective-permute-done | bytes 114720 | tf_op jit(solution)/shard_map/ppermute | solution.py:233
  72.7 3.2 %collective-permute-done.32.refs_1_ = bf16[16,3584]{1,0:T(8,128)(2,1)S(1)} collective-permute-done((bf16[16,3584]{1,0:T(8,128)(2,1)S(1)}, bf16[16,3584]{1,0:T(8,128)(2,1)S(1)}, u32[]{:S(2)}, u32[]{:S(2)}) %collective-permute-start.32) | collective-permute-done | bytes 114720 | tf_op jit(solution)/shard_map/ppermute | solution.py:233
  (83 shorter events, 16.7 us)
Async XLA Ops:
  1.7 9.4 %collective-permute-start = (bf16[16,3712]{1,0:T(8,128)(2,1)}, bf16[16,3712]{1,0:T(8,128)(2,1)S(1)}, u32[]{:S(2)}, u32[]{:S(2)}) collective-permute-start(bf16[16,3712]{1,0:T(8,128)(2,1)} %pack.1.refs_0_), channel_id=1, source_target_pairs={{0,24},{1,25},{2,26},{3,27},{4,28},{5,29},{6,30},{7,31},{8,16},{9,... | collective-permute-start | bytes 356360 | tf_op jit(solution)/shard_map/ppermute | solution.py:230
  6.7 10.2 %collective-permute-start.19 = (bf16[16,3712]{1,0:T(8,128)(2,1)}, bf16[16,3712]{1,0:T(8,128)(2,1)S(1)}, u32[]{:S(2)}, u32[]{:S(2)}) collective-permute-start(bf16[16,3712]{1,0:T(8,128)(2,1)} %pack.1.refs_0_), channel_id=1, source_target_pairs={{0,16},{1,17},{2,18},{3,19},{4,20},{5,21},{6,22},{7,23},{8,24},{9,... | collective-permute-start | bytes 356360 | tf_op jit(solution)/shard_map/ppermute | solution.py:230
  6.7 11.7 %collective-permute-start.13 = (bf16[16,3712]{1,0:T(8,128)(2,1)}, bf16[16,3712]{1,0:T(8,128)(2,1)S(1)}, u32[]{:S(2)}, u32[]{:S(2)}) collective-permute-start(bf16[16,3712]{1,0:T(8,128)(2,1)} %pack.1.refs_0_), channel_id=1, source_target_pairs={{0,8},{1,9},{2,10},{3,11},{4,12},{5,13},{6,14},{7,15},{8,0},{9,1},... | collective-permute-start | bytes 356360 | tf_op jit(solution)/shard_map/ppermute | solution.py:230
  11.1 7.9 %collective-permute-start.1 = (bf16[16,3712]{1,0:T(8,128)(2,1)S(1)}, bf16[16,3712]{1,0:T(8,128)(2,1)S(1)}, u32[]{:S(2)}, u32[]{:S(2)}) collective-permute-start(bf16[16,3712]{1,0:T(8,128)(2,1)S(1)} %collective-permute-done.refs_0_), channel_id=1, source_target_pairs={{0,2},{1,5},{2,0},{3,7},{4,6},{5,1},{6,4},{7,3},{8,10},{9,13},{10,... | collective-permute-start | bytes 356360 | tf_op jit(solution)/shard_map/ppermute | solution.py:230
  12.8 20.6 %collective-permute-start.8 = (bf16[16,3712]{1,0:T(8,128)(2,1)}, bf16[16,3712]{1,0:T(8,128)(2,1)S(1)}, u32[]{:S(2)}, u32[]{:S(2)}) collective-permute-start(bf16[16,3712]{1,0:T(8,128)(2,1)} %pack.1.refs_0_), channel_id=1, source_target_pairs={{0,2},{1,5},{2,0},{3,7},{4,6},{5,1},{6,4},{7,3},{8,10},{9,13},{10,... | collective-permute-start | bytes 356360 | tf_op jit(solution)/shard_map/ppermute | solution.py:230
  13.2 12.9 %collective-permute-start.3 = (bf16[16,3712]{1,0:T(8,128)(2,1)S(1)}, bf16[16,3712]{1,0:T(8,128)(2,1)S(1)}, u32[]{:S(2)}, u32[]{:S(2)}) collective-permute-start(bf16[16,3712]{1,0:T(8,128)(2,1)S(1)} %collective-permute-done.refs_0_), channel_id=1, source_target_pairs={{0,1},{1,0},{2,3},{3,2},{4,5},{5,4},{6,7},{7,6},{8,9},{9,8},{10,11... | collective-permute-start | bytes 356360 | tf_op jit(solution)/shard_map/ppermute | solution.py:230
  18.4 7.2 %collective-permute-start.14 = (bf16[16,3712]{1,0:T(8,128)(2,1)S(1)}, bf16[16,3712]{1,0:T(8,128)(2,1)S(1)}, u32[]{:S(2)}, u32[]{:S(2)}) collective-permute-start(bf16[16,3712]{1,0:T(8,128)(2,1)S(1)} %collective-permute-done.13.refs_0_), channel_id=1, source_target_pairs={{0,2},{1,5},{2,0},{3,7},{4,6},{5,1},{6,4},{7,3},{8,10},{9,13},{10,... | collective-permute-start | bytes 356360 | tf_op jit(solution)/shard_map/ppermute | solution.py:230
  19.0 6.6 %collective-permute-start.2 = (bf16[32,3712]{1,0:T(8,128)(2,1)S(1)}, bf16[32,3712]{1,0:T(8,128)(2,1)S(1)}, u32[]{:S(2)}, u32[]{:S(2)}) collective-permute-start(bf16[32,3712]{1,0:T(8,128)(2,1)S(1)} %pad_maximum_fusion), channel_id=1, source_target_pairs={{0,4},{1,3},{2,6},{3,1},{4,0},{5,7},{6,2},{7,5},{8,12},{9,11},{10,... | collective-permute-start | bytes 712712 | tf_op jit(solution)/shard_map/ppermute | solution.py:230
  23.1 11.7 %collective-permute-start.21 = (bf16[32,3712]{1,0:T(8,128)(2,1)S(1)}, bf16[32,3712]{1,0:T(8,128)(2,1)S(1)}, u32[]{:S(2)}, u32[]{:S(2)}) collective-permute-start(bf16[32,3712]{1,0:T(8,128)(2,1)S(1)} %pad_maximum_fusion.3), channel_id=1, source_target_pairs={{0,4},{1,3},{2,6},{3,1},{4,0},{5,7},{6,2},{7,5},{8,12},{9,11},{10,... | collective-permute-start | bytes 712712 | tf_op jit(solution)/shard_map/ppermute | solution.py:230
  26.1 9.2 %collective-permute-start.15 = (bf16[32,3712]{1,0:T(8,128)(2,1)S(1)}, bf16[32,3712]{1,0:T(8,128)(2,1)S(1)}, u32[]{:S(2)}, u32[]{:S(2)}) collective-permute-start(bf16[32,3712]{1,0:T(8,128)(2,1)S(1)} %pad_maximum_fusion.2), channel_id=1, source_target_pairs={{0,4},{1,3},{2,6},{3,1},{4,0},{5,7},{6,2},{7,5},{8,12},{9,11},{10,... | collective-permute-start | bytes 712712 | tf_op jit(solution)/shard_map/ppermute | solution.py:230
  33.4 6.2 %collective-permute-start.9 = (bf16[32,3712]{1,0:T(8,128)(2,1)S(1)}, bf16[32,3712]{1,0:T(8,128)(2,1)S(1)}, u32[]{:S(2)}, u32[]{:S(2)}) collective-permute-start(bf16[32,3712]{1,0:T(8,128)(2,1)S(1)} %pad_maximum_fusion.1), channel_id=1, source_target_pairs={{0,4},{1,3},{2,6},{3,1},{4,0},{5,7},{6,2},{7,5},{8,12},{9,11},{10,... | collective-permute-start | bytes 712712 | tf_op jit(solution)/shard_map/ppermute | solution.py:230
  35.7 8.2 %collective-permute-start.18 = (bf16[32,3712]{1,0:T(8,128)(2,1)S(1)}, bf16[32,3712]{1,0:T(8,128)(2,1)S(1)}, u32[]{:S(2)}, u32[]{:S(2)}) collective-permute-start(bf16[32,3712]{1,0:T(8,128)(2,1)S(1)} %collective-permute-done.15.refs_2_), channel_id=1, source_target_pairs={{0,1},{1,0},{2,3},{3,2},{4,5},{5,4},{6,7},{7,6},{8,9},{9,8},{10,11... | collective-permute-start | bytes 712712 | tf_op jit(solution)/shard_map/ppermute | solution.py:230
  36.5 6.8 %collective-permute-start.16 = (bf16[16,3712]{1,0:T(8,128)(2,1)S(1)}, bf16[16,3712]{1,0:T(8,128)(2,1)S(1)}, u32[]{:S(2)}, u32[]{:S(2)}) collective-permute-start(bf16[16,3712]{1,0:T(8,128)(2,1)S(1)} %collective-permute-done.13.refs_0_), channel_id=1, source_target_pairs={{0,1},{1,0},{2,3},{3,2},{4,5},{5,4},{6,7},{7,6},{8,9},{9,8},{10,11... | collective-permute-start | bytes 356360 | tf_op jit(solution)/shard_map/ppermute | solution.py:230
  36.8 6.9 %collective-permute-start.17 = (bf16[16,3712]{1,0:T(8,128)(2,1)S(1)}, bf16[16,3712]{1,0:T(8,128)(2,1)S(1)}, u32[]{:S(2)}, u32[]{:S(2)}) collective-permute-start(bf16[16,3712]{1,0:T(8,128)(2,1)S(1)} %collective-permute-done.14.refs_1_), channel_id=1, source_target_pairs={{0,1},{1,0},{2,3},{3,2},{4,5},{5,4},{6,7},{7,6},{8,9},{9,8},{10,11... | collective-permute-start | bytes 356360 | tf_op jit(solution)/shard_map/ppermute | solution.py:230
  39.6 7.4 %collective-permute-start.12 = (bf16[32,3712]{1,0:T(8,128)(2,1)S(1)}, bf16[32,3712]{1,0:T(8,128)(2,1)S(1)}, u32[]{:S(2)}, u32[]{:S(2)}) collective-permute-start(bf16[32,3712]{1,0:T(8,128)(2,1)S(1)} %collective-permute-done.9.refs_2_), channel_id=1, source_target_pairs={{0,1},{1,0},{2,3},{3,2},{4,5},{5,4},{6,7},{7,6},{8,9},{9,8},{10,11... | collective-permute-start | bytes 712712 | tf_op jit(solution)/shard_map/ppermute | solution.py:230
  39.6 7.1 %collective-permute-start.7 = (bf16[32,3584]{1,0:T(8,128)(2,1)S(1)}, bf16[32,3584]{1,0:T(8,128)(2,1)S(1)}, u32[]{:S(2)}, u32[]{:S(2)}) collective-permute-start(bf16[32,3584]{1,0:T(8,128)(2,1)S(1)} %sum_second.4), channel_id=1, source_target_pairs={{4,0},{3,1},{6,2},{1,3},{0,4},{7,5},{2,6},{5,7},{12,8},{11,9},{14,... | collective-permute-start | bytes 688136 | tf_op jit(solution)/shard_map/ppermute | solution.py:233
  46.7 7.1 %collective-permute-start.29 = (bf16[64,3584]{1,0:T(8,128)(2,1)S(1)}, bf16[64,3584]{1,0:T(8,128)(2,1)S(1)}, u32[]{:S(2)}, u32[]{:S(2)}) collective-permute-start(bf16[64,3584]{1,0:T(8,128)(2,1)S(1)} %get-tuple-element.43), channel_id=1, source_target_pairs={{0,1},{1,0},{2,3},{3,2},{4,5},{5,4},{6,7},{7,6},{8,9},{9,8},{10,11... | collective-permute-start | bytes 1376264 | tf_op jit(solution)/shard_map/ppermute | solution.py:230
  52.3 7.3 %collective-permute-start.34 = (bf16[32,3584]{1,0:T(8,128)(2,1)S(1)}, bf16[32,3584]{1,0:T(8,128)(2,1)S(1)}, u32[]{:S(2)}, u32[]{:S(2)}) collective-permute-start(bf16[32,3584]{1,0:T(8,128)(2,1)S(1)} %sum_second.7), channel_id=1, source_target_pairs={{4,0},{3,1},{6,2},{1,3},{0,4},{7,5},{2,6},{5,7},{12,8},{11,9},{14,... | collective-permute-start | bytes 688136 | tf_op jit(solution)/shard_map/ppermute | solution.py:233
  53.8 9.7 %collective-permute-start.30 = (bf16[32,3584]{1,0:T(8,128)(2,1)S(1)}, bf16[32,3584]{1,0:T(8,128)(2,1)S(1)}, u32[]{:S(2)}, u32[]{:S(2)}) collective-permute-start(bf16[32,3584]{1,0:T(8,128)(2,1)S(1)} %sum_second.6), channel_id=1, source_target_pairs={{4,0},{3,1},{6,2},{1,3},{0,4},{7,5},{2,6},{5,7},{12,8},{11,9},{14,... | collective-permute-start | bytes 688136 | tf_op jit(solution)/shard_map/ppermute | solution.py:233
  54.5 6.4 %collective-permute-start.27 = (bf16[16,3584]{1,0:T(8,128)(2,1)S(1)}, bf16[16,3584]{1,0:T(8,128)(2,1)S(1)}, u32[]{:S(2)}, u32[]{:S(2)}) collective-permute-start(bf16[16,3584]{1,0:T(8,128)(2,1)S(1)} %sum_first.4), channel_id=1, source_target_pairs={{2,0},{5,1},{0,2},{7,3},{6,4},{1,5},{4,6},{3,7},{10,8},{13,9},{8,1... | collective-permute-start | bytes 344072 | tf_op jit(solution)/shard_map/ppermute | solution.py:233
  55.8 11.2 %collective-permute-start.26 = (bf16[32,3584]{1,0:T(8,128)(2,1)S(1)}, bf16[32,3584]{1,0:T(8,128)(2,1)S(1)}, u32[]{:S(2)}, u32[]{:S(2)}) collective-permute-start(bf16[32,3584]{1,0:T(8,128)(2,1)S(1)} %sum_second.5), channel_id=1, source_target_pairs={{4,0},{3,1},{6,2},{1,3},{0,4},{7,5},{2,6},{5,7},{12,8},{11,9},{14,... | collective-permute-start | bytes 688136 | tf_op jit(solution)/shard_map/ppermute | solution.py:233
  61.0 6.8 %collective-permute-start.28 = (bf16[16,3584]{1,0:T(8,128)(2,1)S(1)}, bf16[16,3584]{1,0:T(8,128)(2,1)S(1)}, u32[]{:S(2)}, u32[]{:S(2)}) collective-permute-start(bf16[16,3584]{1,0:T(8,128)(2,1)S(1)} %sum_far.4), channel_id=1, source_target_pairs={{24,0},{25,1},{26,2},{27,3},{28,4},{29,5},{30,6},{31,7},{16,8},{17... | collective-permute-start | bytes 344072 | tf_op jit(solution)/shard_map/ppermute | solution.py:233
  65.0 7.7 %collective-permute-start.36 = (bf16[16,3584]{1,0:T(8,128)(2,1)S(1)}, bf16[16,3584]{1,0:T(8,128)(2,1)S(1)}, u32[]{:S(2)}, u32[]{:S(2)}) collective-permute-start(bf16[16,3584]{1,0:T(8,128)(2,1)S(1)} %sum_far.6), channel_id=1, source_target_pairs={{8,0},{9,1},{10,2},{11,3},{12,4},{13,5},{14,6},{15,7},{0,8},{1,9},... | collective-permute-start | bytes 344072 | tf_op jit(solution)/shard_map/ppermute | solution.py:233
  68.8 7.1 %collective-permute-start.32 = (bf16[16,3584]{1,0:T(8,128)(2,1)S(1)}, bf16[16,3584]{1,0:T(8,128)(2,1)S(1)}, u32[]{:S(2)}, u32[]{:S(2)}) collective-permute-start(bf16[16,3584]{1,0:T(8,128)(2,1)S(1)} %sum_far.5), channel_id=1, source_target_pairs={{16,0},{17,1},{18,2},{19,3},{20,4},{21,5},{22,6},{23,7},{24,8},{25... | collective-permute-start | bytes 344072 | tf_op jit(solution)/shard_map/ppermute | solution.py:233
  (18 other events, 68.4 us)

commit v4 on v3

--- a/solution.py
+++ b/solution.py
@@ -260,7 +260,8 @@
         turn = jnp.where(other, 1 - core, core)
         return (place == 0) | (place == 1 + turn)
 
-    order = list(range(far - 1, -1, -1))
+    order = [*range(far - 1, 1, -1), *range(min(far, 2))]
+    assert far > 1
     far_route = {k: routes.along_far(k) for k in range(1, far)}
     many = len(first) + 1
     head, parts, others, pair, out = {}, {}, {}, {}, {}
@@ -270,7 +271,8 @@
         parts[k] = [head[k]] + [routes.send(head[k], r) for r in first]
         if second is not None:
             parts[k].append(routes.send(jnp.concatenate(parts[k], axis=0), second))
-        others[k] = [routes.send(p, cross) for p in parts[k]]
+        parts[k] = [jnp.concatenate(parts[k], axis=0)]
+        others[k] = [routes.send(parts[k][0], cross)]
 
     came = {k: [] for k in order}
     home = {k: [] for k in order}
@@ -311,29 +313,29 @@
     def tie(a, b):
         return lax.optimization_barrier((a, b))
 
+    lead, end = order[0], order[-1]
     for k in order[:-1]:
         compute(k)
         sum_second(k)
         send_second(k)
-    lead = order[0]
     sum_first(lead)
-    parts[0][0], out[lead][0] = tie(parts[0][0], out[lead][0])
+    parts[end][0], out[lead][0] = tie(parts[end][0], out[lead][0])
     send_first(lead)
-    compute(0)
-    sum_second(0)
+    compute(end)
+    sum_second(end)
     sum_far(lead)
     send_far(lead)
-    send_second(0)
+    send_second(end)
     for k in order[1:-1]:
         sum_first(k)
         send_first(k)
         sum_far(k)
         send_far(k)
-    sum_first(0)
-    out[0][0], last[0] = tie(out[0][0], last[0])
-    send_first(0)
-    sum_far(0)
-    send_far(0)
+    sum_first(end)
+    out[end][0], last[0] = tie(out[end][0], last[0])
+    send_first(end)
+    sum_far(end)
+    send_far(end)
     return sums([(a, 0) for a in last], rows, jnp.bfloat16, "sum_last")
 
 

time: 76.7 us -> 73.9 us (0.963)
  starting transfers between devices: 34.6 us -> 32.5 us
  waiting for transfers between devices: 23.4 us -> 21.9 us
  other arithmetic: 0.17 us -> 1.12 us
    ppermute x27 -> x19, starting transfers between devices: 19.5 us -> 17.5 us  [send(): return lax.ppermute(x, self.axes, list(enumerate(route)))]
    ppermute x27 -> x19, waiting for transfers between devices: 14.1 us -> 12.4 us  [send(): return lax.ppermute(x, self.axes, list(enumerate(route)))]
    concatenate x4, other arithmetic: 0.1 us -> 1 us  [per_device(): parts[k].append(routes.send(jnp.concatenate(parts[k], axis=0), second))]
  transfers between devices with their start and end apart: 38 -> 30, of which waited for: 12 -> 11; matrix products, arithmetic and copies ran while one was open for 0% -> 2% of each run, Pallas kernels for 19% -> 20%
where the time goes in v4:
time: 73.9 us; the launch traced here: 73.7 us
  starting transfers between devices  32.5 us (44%)
  waiting for transfers between devices  21.9 us (30%)
  Pallas kernels  17.1 us (23%)
  other arithmetic  1.12 us (2%)
  local copies, waits for them, and re-layouts  0.81 us (1%)
    ppermute x19, starting transfers between devices, send(): return lax.ppermute(x, self.axes, list(enumerate(route)))  17.5 us
    ppermute x11, starting transfers between devices, send_back(): lax.ppermute(x, self.axes, [(to, fro) for fro, to in enumerate(route)])  15 us
    pallas_call x4, Pallas kernels, ffn(): pl.pallas_call(functools.partial(ffn_body, len(own_parts), len(weights),...  14.1 us
    ppermute x19, waiting for transfers between devices, send(): return lax.ppermute(x, self.axes, list(enumerate(route)))  12.4 us
    ppermute x11, waiting for transfers between devices, send_back(): lax.ppermute(x, self.axes, [(to, fro) for fro, to in enumerate(route)])  9.56 us
    pallas_call x1, Pallas kernels, pack(): pl.pallas_call(pack_body, out_shape=jax.ShapeDtypeStruct((rows, model + w...  1.66 us
  transfers between devices with their start and end apart: 30, of which 11 were waited for; matrix products, arithmetic and copies ran while one was open for 2% of the time, Pallas kernels for 20%

profile of v4, /device:TPU:0, one launch (start us, length us, event | category | flops | bytes accessed | tf_op | source)
XLA Modules:
  0.0 73.7 jit_solution(17905849042292846686)
XLA Ops:
  0.0 1.7 %pack.1 = bf16[16,3712]{1,0:T(8,128)(2,1)} custom-call(bf16[16,3584]{1,0:T(8,128)(2,1)} %tokens_ref.1, s32[8,16]{1,0:T(8,128)} %bitcast.10, f32[8,16]{1,0:T(8,128)} %bitcast.11), custom_call_target="tpu_custom_call" | custom-call | tf_op jit(solution)/shard_map/pack/pallas_call | solution.py:43
  1.7 2.9 %collective-permute-start.10 = (bf16[16,3712]{1,0:T(8,128)(2,1)}, bf16[16,3712]{1,0:T(8,128)(2,1)S(1)}, u32[]{:S(2)}, u32[]{:S(2)}) collective-permute-start(bf16[16,3712]{1,0:T(8,128)(2,1)} %pack.1), channel_id=1, source_target_pairs={{0,2},{1,5},{2,0},{3,7},{4,6},{5,1},{6,4},{7,3},{8,10},{9,13},{10,... | collective-permute-start | bytes 356360 | tf_op jit(solution)/shard_map/ppermute | solution.py:230
  4.6 3.6 %collective-permute-start.3 = (bf16[16,3712]{1,0:T(8,128)(2,1)}, bf16[16,3712]{1,0:T(8,128)(2,1)S(1)}, u32[]{:S(2)}, u32[]{:S(2)}) collective-permute-start(bf16[16,3712]{1,0:T(8,128)(2,1)} %pack.1), channel_id=1, source_target_pairs={{0,24},{1,25},{2,26},{3,27},{4,28},{5,29},{6,30},{7,31},{8,16},{9,... | collective-permute-start | bytes 356360 | tf_op jit(solution)/shard_map/ppermute | solution.py:230
  10.0 1.6 %collective-permute-start.11 = (bf16[32,3712]{1,0:T(8,128)(2,1)S(1)}, bf16[32,3712]{1,0:T(8,128)(2,1)S(1)}, u32[]{:S(2)}, u32[]{:S(2)}) collective-permute-start(bf16[32,3712]{1,0:T(8,128)(2,1)S(1)} %pad_maximum_fusion.3), channel_id=1, source_target_pairs={{0,4},{1,3},{2,6},{3,1},{4,0},{5,7},{6,2},{7,5},{8,12},{9,11},{10,... | collective-permute-start | bytes 712712 | tf_op jit(solution)/shard_map/ppermute | solution.py:230
  11.6 1.2 %collective-permute-done.3 = bf16[16,3712]{1,0:T(8,128)(2,1)S(1)} collective-permute-done((bf16[16,3712]{1,0:T(8,128)(2,1)}, bf16[16,3712]{1,0:T(8,128)(2,1)S(1)}, u32[]{:S(2)}, u32[]{:S(2)}) %collective-permute-start.3) | collective-permute-done | bytes 118816 | tf_op jit(solution)/shard_map/ppermute | solution.py:230
  13.1 1.8 %collective-permute-done = bf16[16,3712]{1,0:T(8,128)(2,1)S(1)} collective-permute-done((bf16[16,3712]{1,0:T(8,128)(2,1)}, bf16[16,3712]{1,0:T(8,128)(2,1)S(1)}, u32[]{:S(2)}, u32[]{:S(2)}) %collective-permute-start) | collective-permute-done | bytes 118816 | tf_op jit(solution)/shard_map/ppermute | solution.py:230
  15.0 1.6 %collective-permute-start.1 = (bf16[16,3712]{1,0:T(8,128)(2,1)S(1)}, bf16[16,3712]{1,0:T(8,128)(2,1)S(1)}, u32[]{:S(2)}, u32[]{:S(2)}) collective-permute-start(bf16[16,3712]{1,0:T(8,128)(2,1)S(1)} %collective-permute-done), channel_id=1, source_target_pairs={{0,2},{1,5},{2,0},{3,7},{4,6},{5,1},{6,4},{7,3},{8,10},{9,13},{10,... | collective-permute-start | bytes 356360 | tf_op jit(solution)/shard_map/ppermute | solution.py:230
  16.6 1.6 %collective-permute-done.13 = bf16[16,3712]{1,0:T(8,128)(2,1)S(1)} collective-permute-done((bf16[16,3712]{1,0:T(8,128)(2,1)}, bf16[16,3712]{1,0:T(8,128)(2,1)S(1)}, u32[]{:S(2)}, u32[]{:S(2)}) %collective-permute-start.13) | collective-permute-done | bytes 118816 | tf_op jit(solution)/shard_map/ppermute | solution.py:230
  18.2 1.5 %collective-permute-start.14 = (bf16[16,3712]{1,0:T(8,128)(2,1)S(1)}, bf16[16,3712]{1,0:T(8,128)(2,1)S(1)}, u32[]{:S(2)}, u32[]{:S(2)}) collective-permute-start(bf16[16,3712]{1,0:T(8,128)(2,1)S(1)} %collective-permute-done.13), channel_id=1, source_target_pairs={{0,2},{1,5},{2,0},{3,7},{4,6},{5,1},{6,4},{7,3},{8,10},{9,13},{10,... | collective-permute-start | bytes 356360 | tf_op jit(solution)/shard_map/ppermute | solution.py:230
  20.3 1.6 %collective-permute-start.2 = (bf16[32,3712]{1,0:T(8,128)(2,1)S(1)}, bf16[32,3712]{1,0:T(8,128)(2,1)S(1)}, u32[]{:S(2)}, u32[]{:S(2)}) collective-permute-start(bf16[32,3712]{1,0:T(8,128)(2,1)S(1)} %pad_maximum_fusion.1), channel_id=1, source_target_pairs={{0,4},{1,3},{2,6},{3,1},{4,0},{5,7},{6,2},{7,5},{8,12},{9,11},{10,... | collective-permute-start | bytes 712712 | tf_op jit(solution)/shard_map/ppermute | solution.py:230
  21.9 2.4 %collective-permute-done.14 = bf16[16,3712]{1,0:T(8,128)(2,1)S(1)} collective-permute-done((bf16[16,3712]{1,0:T(8,128)(2,1)S(1)}, bf16[16,3712]{1,0:T(8,128)(2,1)S(1)}, u32[]{:S(2)}, u32[]{:S(2)}) %collective-permute-start.14) | collective-permute-done | bytes 118816 | tf_op jit(solution)/shard_map/ppermute | solution.py:230
  26.6 4.4 %collective-permute-done.15 = bf16[32,3712]{1,0:T(8,128)(2,1)S(1)} collective-permute-done((bf16[32,3712]{1,0:T(8,128)(2,1)S(1)}, bf16[32,3712]{1,0:T(8,128)(2,1)S(1)}, u32[]{:S(2)}, u32[]{:S(2)}) %collective-permute-start.15) | collective-permute-done | bytes 237600 | tf_op jit(solution)/shard_map/ppermute | solution.py:230
  31.1 5.5 %ffn_3.1 = (bf16[64,3584]{1,0:T(8,128)(2,1)S(1)}, bf16[64,3584]{1,0:T(8,128)(2,1)S(1)}, bf16[3584,512]{1,0:T(8,128)(2,1)S(1)}, bf16[3584,512]{1,0:T(8,128)(2,1)S(1)}, bf16[512,3584]{1,0:T(8,128)(2,1)S(1)}) custom-call(s32[2]{0:T(128)S(1)} %pad_add_fusion.index_ref, bf16[64,3712]{1,0:T(8,128)(2,1)S(1)} %constant_dynamic-update-slice_fusion.3.refs_0_, ...), custom_call_target="tpu_custom_call" | custom-call | flops 1409286144 | bytes 1835008 | tf_op jit(solution)/shard_map/ffn_3/pallas_call | solution.py:131
  37.3 2.3 %ffn_2.1 = (bf16[64,3584]{1,0:T(8,128)(2,1)S(1)}, bf16[64,3584]{1,0:T(8,128)(2,1)S(1)}, bf16[3584,512]{1,0:T(8,128)(2,1)S(1)}, bf16[3584,512]{1,0:T(8,128)(2,1)S(1)}, bf16[512,3584]{1,0:T(8,128)(2,1)S(1)}) custom-call(s32[2]{0:T(128)S(1)} %pad_add_fusion.index_ref, ...), custom_call_target="tpu_custom_call", output_to_operand_aliasing={{2}: (3, {}), {3}: (4, {}), {4}: (5, {})} | custom-call | flops 1409286144 | bytes 1835008 | tf_op jit(solution)/shard_map/ffn_2/pallas_call | solution.py:131
  41.5 3.9 %ffn_0.1 = (bf16[64,3584]{1,0:T(8,128)(2,1)S(1)}, bf16[64,3584]{1,0:T(8,128)(2,1)S(1)}, bf16[3584,512]{1,0:T(8,128)(2,1)S(1)}, bf16[3584,512]{1,0:T(8,128)(2,1)S(1)}, bf16[512,3584]{1,0:T(8,128)(2,1)S(1)}) custom-call(s32[2]{0:T(128)S(1)} %pad_add_fusion.index_ref, ...), custom_call_target="tpu_custom_call", output_to_operand_aliasing={{2}: (3, {}), {3}: (4, {}), {4}: (5, {})} | custom-call | flops 2818572288 | bytes 1835008 | tf_op jit(solution)/shard_map/ffn_0/pallas_call | solution.py:131
  46.4 2.3 %ffn_1.1 = (bf16[64,3584]{1,0:T(8,128)(2,1)S(1)}, bf16[64,3584]{1,0:T(8,128)(2,1)S(1)}, bf16[3584,512]{1,0:T(8,128)(2,1)S(1)}, bf16[3584,512]{1,0:T(8,128)(2,1)S(1)}, bf16[512,3584]{1,0:T(8,128)(2,1)S(1)}) custom-call(s32[2]{0:T(128)S(1)} %pad_add_fusion.index_ref, ...), custom_call_target="tpu_custom_call", output_to_operand_aliasing={{2}: (3, {}), {3}: (4, {}), {4}: (5, {})} | custom-call | flops 1409286144 | bytes 1835008 | tf_op jit(solution)/shard_map/ffn_1/pallas_call | solution.py:131
  50.9 1.7 %collective-permute-start.18 = (bf16[32,3584]{1,0:T(8,128)(2,1)S(1)}, bf16[32,3584]{1,0:T(8,128)(2,1)S(1)}, u32[]{:S(2)}, u32[]{:S(2)}) collective-permute-start(bf16[32,3584]{1,0:T(8,128)(2,1)S(1)} %sum_second.5), channel_id=1, source_target_pairs={{4,0},{3,1},{6,2},{1,3},{0,4},{7,5},{2,6},{5,7},{12,8},{11,9},{14,... | collective-permute-start | bytes 688136 | tf_op jit(solution)/shard_map/ppermute | solution.py:233
  53.1 3.0 %collective-permute-done.19.refs_3_ = bf16[16,3584]{1,0:T(8,128)(2,1)S(1)} collective-permute-done((bf16[16,3584]{1,0:T(8,128)(2,1)S(1)}, bf16[16,3584]{1,0:T(8,128)(2,1)S(1)}, u32[]{:S(2)}, u32[]{:S(2)}) %collective-permute-start.19) | collective-permute-done | bytes 114720 | tf_op jit(solution)/shard_map/ppermute | solution.py:233
  56.1 2.7 %collective-permute-start.20 = (bf16[16,3584]{1,0:T(8,128)(2,1)S(1)}, bf16[16,3584]{1,0:T(8,128)(2,1)S(1)}, u32[]{:S(2)}, u32[]{:S(2)}) collective-permute-start(bf16[16,3584]{1,0:T(8,128)(2,1)S(1)} %sum_far.4), channel_id=1, source_target_pairs={{24,0},{25,1},{26,2},{27,3},{28,4},{29,5},{30,6},{31,7},{16,8},{17... | collective-permute-start | bytes 344072 | tf_op jit(solution)/shard_map/ppermute | solution.py:233
  60.0 2.8 %collective-permute-done.20.refs_0_ = bf16[16,3584]{1,0:T(8,128)(2,1)S(1)} collective-permute-done((bf16[16,3584]{1,0:T(8,128)(2,1)S(1)}, bf16[16,3584]{1,0:T(8,128)(2,1)S(1)}, u32[]{:S(2)}, u32[]{:S(2)}) %collective-permute-start.20) | collective-permute-done | bytes 114720 | tf_op jit(solution)/shard_map/ppermute | solution.py:233
  63.7 1.2 %collective-permute-start.27 = (bf16[16,3584]{1,0:T(8,128)(2,1)S(1)}, bf16[16,3584]{1,0:T(8,128)(2,1)S(1)}, u32[]{:S(2)}, u32[]{:S(2)}) collective-permute-start(bf16[16,3584]{1,0:T(8,128)(2,1)S(1)} %sum_first.7), channel_id=1, source_target_pairs={{2,0},{5,1},{0,2},{7,3},{6,4},{1,5},{4,6},{3,7},{10,8},{13,9},{8,1... | collective-permute-start | bytes 344072 | tf_op jit(solution)/shard_map/ppermute | solution.py:233
  65.0 2.6 %collective-permute-start.24 = (bf16[16,3584]{1,0:T(8,128)(2,1)S(1)}, bf16[16,3584]{1,0:T(8,128)(2,1)S(1)}, u32[]{:S(2)}, u32[]{:S(2)}) collective-permute-start(bf16[16,3584]{1,0:T(8,128)(2,1)S(1)} %sum_far.5), channel_id=1, source_target_pairs={{16,0},{17,1},{18,2},{19,3},{20,4},{21,5},{22,6},{23,7},{24,8},{25... | collective-permute-start | bytes 344072 | tf_op jit(solution)/shard_map/ppermute | solution.py:233
  67.7 2.4 %collective-permute-start.29 = (bf16[16,3584]{1,0:T(8,128)(2,1)S(1)}, bf16[16,3584]{1,0:T(8,128)(2,1)S(1)}, u32[]{:S(2)}, u32[]{:S(2)}) collective-permute-start(bf16[16,3584]{1,0:T(8,128)(2,1)S(1)} %sum_far.7), channel_id=1, source_target_pairs={{8,0},{9,1},{10,2},{11,3},{12,4},{13,5},{14,6},{15,7},{0,8},{1,9},... | collective-permute-start | bytes 344072 | tf_op jit(solution)/shard_map/ppermute | solution.py:233
  70.2 1.8 %collective-permute-done.24.refs_1_ = bf16[16,3584]{1,0:T(8,128)(2,1)S(1)} collective-permute-done((bf16[16,3584]{1,0:T(8,128)(2,1)S(1)}, bf16[16,3584]{1,0:T(8,128)(2,1)S(1)}, u32[]{:S(2)}, u32[]{:S(2)}) %collective-permute-start.24) | collective-permute-done | bytes 114720 | tf_op jit(solution)/shard_map/ppermute | solution.py:233
  (77 shorter events, 15.3 us)
Async XLA Ops:
  1.7 7.4 %collective-permute-start.10 = (bf16[16,3712]{1,0:T(8,128)(2,1)}, bf16[16,3712]{1,0:T(8,128)(2,1)S(1)}, u32[]{:S(2)}, u32[]{:S(2)}) collective-permute-start(bf16[16,3712]{1,0:T(8,128)(2,1)} %pack.1), channel_id=1, source_target_pairs={{0,2},{1,5},{2,0},{3,7},{4,6},{5,1},{6,4},{7,3},{8,10},{9,13},{10,... | collective-permute-start | bytes 356360 | tf_op jit(solution)/shard_map/ppermute | solution.py:230
  4.6 8.2 %collective-permute-start.3 = (bf16[16,3712]{1,0:T(8,128)(2,1)}, bf16[16,3712]{1,0:T(8,128)(2,1)S(1)}, u32[]{:S(2)}, u32[]{:S(2)}) collective-permute-start(bf16[16,3712]{1,0:T(8,128)(2,1)} %pack.1), channel_id=1, source_target_pairs={{0,24},{1,25},{2,26},{3,27},{4,28},{5,29},{6,30},{7,31},{8,16},{9,... | collective-permute-start | bytes 356360 | tf_op jit(solution)/shard_map/ppermute | solution.py:230
  8.2 6.8 %collective-permute-start = (bf16[16,3712]{1,0:T(8,128)(2,1)}, bf16[16,3712]{1,0:T(8,128)(2,1)S(1)}, u32[]{:S(2)}, u32[]{:S(2)}) collective-permute-start(bf16[16,3712]{1,0:T(8,128)(2,1)} %pack.1), channel_id=1, source_target_pairs={{0,8},{1,9},{2,10},{3,11},{4,12},{5,13},{6,14},{7,15},{8,0},{9,1},... | collective-permute-start | bytes 356360 | tf_op jit(solution)/shard_map/ppermute | solution.py:230
  8.2 10.0 %collective-permute-start.13 = (bf16[16,3712]{1,0:T(8,128)(2,1)}, bf16[16,3712]{1,0:T(8,128)(2,1)S(1)}, u32[]{:S(2)}, u32[]{:S(2)}) collective-permute-start(bf16[16,3712]{1,0:T(8,128)(2,1)} %pack.1), channel_id=1, source_target_pairs={{0,16},{1,17},{2,18},{3,19},{4,20},{5,21},{6,22},{7,23},{8,24},{9,... | collective-permute-start | bytes 356360 | tf_op jit(solution)/shard_map/ppermute | solution.py:230
  10.0 16.0 %collective-permute-start.11 = (bf16[32,3712]{1,0:T(8,128)(2,1)S(1)}, bf16[32,3712]{1,0:T(8,128)(2,1)S(1)}, u32[]{:S(2)}, u32[]{:S(2)}) collective-permute-start(bf16[32,3712]{1,0:T(8,128)(2,1)S(1)} %pad_maximum_fusion.3), channel_id=1, source_target_pairs={{0,4},{1,3},{2,6},{3,1},{4,0},{5,7},{6,2},{7,5},{8,12},{9,11},{10,... | collective-permute-start | bytes 712712 | tf_op jit(solution)/shard_map/ppermute | solution.py:230
  12.8 6.9 %collective-permute-start.4 = (bf16[16,3712]{1,0:T(8,128)(2,1)S(1)}, bf16[16,3712]{1,0:T(8,128)(2,1)S(1)}, u32[]{:S(2)}, u32[]{:S(2)}) collective-permute-start(bf16[16,3712]{1,0:T(8,128)(2,1)S(1)} %collective-permute-done.3), channel_id=1, source_target_pairs={{0,2},{1,5},{2,0},{3,7},{4,6},{5,1},{6,4},{7,3},{8,10},{9,13},{10,... | collective-permute-start | bytes 356360 | tf_op jit(solution)/shard_map/ppermute | solution.py:230
  18.2 6.1 %collective-permute-start.14 = (bf16[16,3712]{1,0:T(8,128)(2,1)S(1)}, bf16[16,3712]{1,0:T(8,128)(2,1)S(1)}, u32[]{:S(2)}, u32[]{:S(2)}) collective-permute-start(bf16[16,3712]{1,0:T(8,128)(2,1)S(1)} %collective-permute-done.13), channel_id=1, source_target_pairs={{0,2},{1,5},{2,0},{3,7},{4,6},{5,1},{6,4},{7,3},{8,10},{9,13},{10,... | collective-permute-start | bytes 356360 | tf_op jit(solution)/shard_map/ppermute | solution.py:230
  19.7 6.2 %collective-permute-start.5 = (bf16[32,3712]{1,0:T(8,128)(2,1)S(1)}, bf16[32,3712]{1,0:T(8,128)(2,1)S(1)}, u32[]{:S(2)}, u32[]{:S(2)}) collective-permute-start(bf16[32,3712]{1,0:T(8,128)(2,1)S(1)} %pad_maximum_fusion.2), channel_id=1, source_target_pairs={{0,4},{1,3},{2,6},{3,1},{4,0},{5,7},{6,2},{7,5},{8,12},{9,11},{10,... | collective-permute-start | bytes 712712 | tf_op jit(solution)/shard_map/ppermute | solution.py:230
  20.3 16.9 %collective-permute-start.2 = (bf16[32,3712]{1,0:T(8,128)(2,1)S(1)}, bf16[32,3712]{1,0:T(8,128)(2,1)S(1)}, u32[]{:S(2)}, u32[]{:S(2)}) collective-permute-start(bf16[32,3712]{1,0:T(8,128)(2,1)S(1)} %pad_maximum_fusion.1), channel_id=1, source_target_pairs={{0,4},{1,3},{2,6},{3,1},{4,0},{5,7},{6,2},{7,5},{8,12},{9,11},{10,... | collective-permute-start | bytes 712712 | tf_op jit(solution)/shard_map/ppermute | solution.py:230
  24.3 6.7 %collective-permute-start.15 = (bf16[32,3712]{1,0:T(8,128)(2,1)S(1)}, bf16[32,3712]{1,0:T(8,128)(2,1)S(1)}, u32[]{:S(2)}, u32[]{:S(2)}) collective-permute-start(bf16[32,3712]{1,0:T(8,128)(2,1)S(1)} %pad_maximum_fusion.4), channel_id=1, source_target_pairs={{0,4},{1,3},{2,6},{3,1},{4,0},{5,7},{6,2},{7,5},{8,12},{9,11},{10,... | collective-permute-start | bytes 712712 | tf_op jit(solution)/shard_map/ppermute | solution.py:230
  26.1 14.8 %collective-permute-start.12 = (bf16[64,3712]{1,0:T(8,128)(2,1)S(1)}, bf16[64,3712]{1,0:T(8,128)(2,1)S(1)}, u32[]{:S(2)}, u32[]{:S(2)}) collective-permute-start(bf16[64,3712]{1,0:T(8,128)(2,1)S(1)} %pad_maximum_fusion.refs_0_), channel_id=1, source_target_pairs={{0,1},{1,0},{2,3},{3,2},{4,5},{5,4},{6,7},{7,6},{8,9},{9,8},{10,11... | collective-permute-start | bytes 1425416 | tf_op jit(solution)/shard_map/ppermute | solution.py:230
  31.0 6.3 %collective-permute-start.16 = (bf16[64,3712]{1,0:T(8,128)(2,1)S(1)}, bf16[64,3712]{1,0:T(8,128)(2,1)S(1)}, u32[]{:S(2)}, u32[]{:S(2)}) collective-permute-start(bf16[64,3712]{1,0:T(8,128)(2,1)S(1)} %constant_dynamic-update-slice_fusion.6.refs_0_), channel_id=1, source_target_pairs={{0,1},{1,0},{2,3},{3,2},{4,5},{5,4},{6,7},{7,6},{8,9},{9,8},{10,11... | collective-permute-start | bytes 1425416 | tf_op jit(solution)/shard_map/ppermute | solution.py:230
  37.2 9.2 %collective-permute-start.9 = (bf16[64,3712]{1,0:T(8,128)(2,1)S(1)}, bf16[64,3712]{1,0:T(8,128)(2,1)S(1)}, u32[]{:S(2)}, u32[]{:S(2)}) collective-permute-start(bf16[64,3712]{1,0:T(8,128)(2,1)S(1)} %constant_dynamic-update-slice_fusion.refs_0_), channel_id=1, source_target_pairs={{0,1},{1,0},{2,3},{3,2},{4,5},{5,4},{6,7},{7,6},{8,9},{9,8},{10,11... | collective-permute-start | bytes 1425416 | tf_op jit(solution)/shard_map/ppermute | solution.py:230
  39.7 9.7 %collective-permute-start.21 = (bf16[64,3584]{1,0:T(8,128)(2,1)S(1)}, bf16[64,3584]{1,0:T(8,128)(2,1)S(1)}, u32[]{:S(2)}, u32[]{:S(2)}) collective-permute-start(bf16[64,3584]{1,0:T(8,128)(2,1)S(1)} %get-tuple-element.43), channel_id=1, source_target_pairs={{0,1},{1,0},{2,3},{3,2},{4,5},{5,4},{6,7},{7,6},{8,9},{9,8},{10,11... | collective-permute-start | bytes 1376264 | tf_op jit(solution)/shard_map/ppermute | solution.py:230
  40.3 6.1 %collective-permute-start.8 = (bf16[32,3584]{1,0:T(8,128)(2,1)S(1)}, bf16[32,3584]{1,0:T(8,128)(2,1)S(1)}, u32[]{:S(2)}, u32[]{:S(2)}) collective-permute-start(bf16[32,3584]{1,0:T(8,128)(2,1)S(1)} %sum_second.4), channel_id=1, source_target_pairs={{4,0},{3,1},{6,2},{1,3},{0,4},{7,5},{2,6},{5,7},{12,8},{11,9},{14,... | collective-permute-start | bytes 688136 | tf_op jit(solution)/shard_map/ppermute | solution.py:233
  49.4 9.4 %collective-permute-start.22 = (bf16[32,3584]{1,0:T(8,128)(2,1)S(1)}, bf16[32,3584]{1,0:T(8,128)(2,1)S(1)}, u32[]{:S(2)}, u32[]{:S(2)}) collective-permute-start(bf16[32,3584]{1,0:T(8,128)(2,1)S(1)} %sum_second.6), channel_id=1, source_target_pairs={{4,0},{3,1},{6,2},{1,3},{0,4},{7,5},{2,6},{5,7},{12,8},{11,9},{14,... | collective-permute-start | bytes 688136 | tf_op jit(solution)/shard_map/ppermute | solution.py:233
  50.0 6.1 %collective-permute-start.19 = (bf16[16,3584]{1,0:T(8,128)(2,1)S(1)}, bf16[16,3584]{1,0:T(8,128)(2,1)S(1)}, u32[]{:S(2)}, u32[]{:S(2)}) collective-permute-start(bf16[16,3584]{1,0:T(8,128)(2,1)S(1)} %sum_first.4), channel_id=1, source_target_pairs={{2,0},{5,1},{0,2},{7,3},{6,4},{1,5},{4,6},{3,7},{10,8},{13,9},{8,1... | collective-permute-start | bytes 344072 | tf_op jit(solution)/shard_map/ppermute | solution.py:233
  50.9 9.1 %collective-permute-start.18 = (bf16[32,3584]{1,0:T(8,128)(2,1)S(1)}, bf16[32,3584]{1,0:T(8,128)(2,1)S(1)}, u32[]{:S(2)}, u32[]{:S(2)}) collective-permute-start(bf16[32,3584]{1,0:T(8,128)(2,1)S(1)} %sum_second.5), channel_id=1, source_target_pairs={{4,0},{3,1},{6,2},{1,3},{0,4},{7,5},{2,6},{5,7},{12,8},{11,9},{14,... | collective-permute-start | bytes 688136 | tf_op jit(solution)/shard_map/ppermute | solution.py:233
  52.7 11.0 %collective-permute-start.26 = (bf16[32,3584]{1,0:T(8,128)(2,1)S(1)}, bf16[32,3584]{1,0:T(8,128)(2,1)S(1)}, u32[]{:S(2)}, u32[]{:S(2)}) collective-permute-start(bf16[32,3584]{1,0:T(8,128)(2,1)S(1)} %sum_second.7), channel_id=1, source_target_pairs={{4,0},{3,1},{6,2},{1,3},{0,4},{7,5},{2,6},{5,7},{12,8},{11,9},{14,... | collective-permute-start | bytes 688136 | tf_op jit(solution)/shard_map/ppermute | solution.py:233
  56.1 6.7 %collective-permute-start.20 = (bf16[16,3584]{1,0:T(8,128)(2,1)S(1)}, bf16[16,3584]{1,0:T(8,128)(2,1)S(1)}, u32[]{:S(2)}, u32[]{:S(2)}) collective-permute-start(bf16[16,3584]{1,0:T(8,128)(2,1)S(1)} %sum_far.4), channel_id=1, source_target_pairs={{24,0},{25,1},{26,2},{27,3},{28,4},{29,5},{30,6},{31,7},{16,8},{17... | collective-permute-start | bytes 344072 | tf_op jit(solution)/shard_map/ppermute | solution.py:233
  58.9 6.1 %collective-permute-start.23 = (bf16[16,3584]{1,0:T(8,128)(2,1)S(1)}, bf16[16,3584]{1,0:T(8,128)(2,1)S(1)}, u32[]{:S(2)}, u32[]{:S(2)}) collective-permute-start(bf16[16,3584]{1,0:T(8,128)(2,1)S(1)} %sum_first.6), channel_id=1, source_target_pairs={{2,0},{5,1},{0,2},{7,3},{6,4},{1,5},{4,6},{3,7},{10,8},{13,9},{8,1... | collective-permute-start | bytes 344072 | tf_op jit(solution)/shard_map/ppermute | solution.py:233
  63.7 6.4 %collective-permute-start.27 = (bf16[16,3584]{1,0:T(8,128)(2,1)S(1)}, bf16[16,3584]{1,0:T(8,128)(2,1)S(1)}, u32[]{:S(2)}, u32[]{:S(2)}) collective-permute-start(bf16[16,3584]{1,0:T(8,128)(2,1)S(1)} %sum_first.7), channel_id=1, source_target_pairs={{2,0},{5,1},{0,2},{7,3},{6,4},{1,5},{4,6},{3,7},{10,8},{13,9},{8,1... | collective-permute-start | bytes 344072 | tf_op jit(solution)/shard_map/ppermute | solution.py:233
  65.0 6.9 %collective-permute-start.24 = (bf16[16,3584]{1,0:T(8,128)(2,1)S(1)}, bf16[16,3584]{1,0:T(8,128)(2,1)S(1)}, u32[]{:S(2)}, u32[]{:S(2)}) collective-permute-start(bf16[16,3584]{1,0:T(8,128)(2,1)S(1)} %sum_far.5), channel_id=1, source_target_pairs={{16,0},{17,1},{18,2},{19,3},{20,4},{21,5},{22,6},{23,7},{24,8},{25... | collective-permute-start | bytes 344072 | tf_op jit(solution)/shard_map/ppermute | solution.py:233
  67.7 5.4 %collective-permute-start.29 = (bf16[16,3584]{1,0:T(8,128)(2,1)S(1)}, bf16[16,3584]{1,0:T(8,128)(2,1)S(1)}, u32[]{:S(2)}, u32[]{:S(2)}) collective-permute-start(bf16[16,3584]{1,0:T(8,128)(2,1)S(1)} %sum_far.7), channel_id=1, source_target_pairs={{8,0},{9,1},{10,2},{11,3},{12,4},{13,5},{14,6},{15,7},{0,8},{1,9},... | collective-permute-start | bytes 344072 | tf_op jit(solution)/shard_map/ppermute | solution.py:233
  (10 other events, 60.3 us)
